TPU v7x, 32 devices: a whole 2x2x4 slice. The times are simulated.
32 devices in a mesh: groups: 2 (over x), tm: 16 (over z, y, core).
Axes of the slice: x: 2, y: 2, z: 4, core: 2. Of those that a mesh axis runs over, the one named last changes fastest.
Arguments:
- pixels: bfloat16 [128, 128, 1536], P(('groups', 'tm')), parts along dimension 0, as said below
- prior_kv: bfloat16 [2, 16, 128, 640], P(None, 'groups'), parts along dimension 1, may hold values from -6 to 6
- w_embed: bfloat16 [1536, 1280], replicated, may hold values from -0.15625 to 0.15625
- ln_gain: float32 [1280], replicated, may hold values from 0.1 to 1.9
- w_query: bfloat16 [1280, 640], replicated, as said below
- w_key: bfloat16 [1280, 640], replicated, as said below
- w_value: bfloat16 [1280, 640], replicated, may hold values from -0.15625 to 0.15625
- w_out: bfloat16 [640, 1280], replicated, may hold values from -0.25 to 0.25
Outputs:
- encoded: bfloat16 [128, 128, 1280], P(('groups', 'tm')), parts along dimension 0
There are 2 independent parts, one for each index of `groups`. A program takes and returns all parts, laid end to end along the dimension named above; an argument that names none is the same for every part. Nothing has to cross between parts.
Inputs may be any that keep to these rules, and one draw needn't show every extreme that they name: `pixels`: standardized pixel values. `w_query`: query projection, entries of order 1280 ** -0.5. `w_key`: key projection.
All inputs are finite; a program needn't handle non-finite values.
Results may differ from a plain program's by a relative error of at most 0.007.
Values may be sent and summed in bfloat16 or wider, within the bound.
No kernel may reach another device: no remote copies, remote signals or barrier semaphores. Data moves between devices by JAX's collectives and lax.ppermute only.
A program may use at most 64 MiB of HBM per device.

v0:
```python
import functools
import math

import jax
import jax.numpy as jnp
from jax import lax
from jax.experimental import pallas as pl
from jax.experimental.pallas import tpu as pltpu
from jax.sharding import PartitionSpec as P

HEADS = 8
HEAD_DIM = 80
BF = jnp.bfloat16
F32 = jnp.float32
ANY = pl.BlockSpec(memory_space=pl.ANY)
HBM = pl.BlockSpec(memory_space=pltpu.HBM)
VMEM = pl.BlockSpec(memory_space=pltpu.VMEM)
MIB = 1 << 20


def params(mib):
    return pltpu.CompilerParams(vmem_limit_bytes=mib * MIB)


COST = {"slice": 1, "front": 37000, "second": 1, "ahead": 1300, "pack_key": 1, "pack_value": 1,
        "score": 1, "mix": 1, "finish": 1}
K_PIECES = 2
V_PIECES = 2


def call(kernel, name, mib, out_shape, in_specs, out_specs, scratch=(), aliases=None):
    return pl.pallas_call(
        kernel,
        out_shape=out_shape,
        in_specs=in_specs,
        out_specs=out_specs,
        scratch_shapes=list(scratch),
        input_output_aliases=aliases or {},
        compiler_params=params(mib),
        cost_estimate=pl.CostEstimate(flops=COST[name] * 10**6, bytes_accessed=1, transcendentals=0),
        name=name,
    )


def shape(dims, dtype=BF):
    return jax.ShapeDtypeStruct(dims, dtype)


def head_rows(h):
    return pl.ds(pl.multiple_of(h * HEAD_DIM, 16), HEAD_DIM)


def normed_rows(emb, part, gain):
    wide = emb[part, :].astype(F32)
    center = wide - jnp.mean(wide, axis=-1, keepdims=True)
    spread = jnp.mean(center * center, axis=-1, keepdims=True)
    return (center * lax.rsqrt(spread + 1e-06) * gain).astype(BF)


def copy_in(pairs, sems):
    copies = [
        pltpu.make_async_copy(source, target, sems.at[i]) for i, (source, target) in enumerate(pairs)
    ]
    for copy in copies:
        copy.start()
    return copies


def position():
    place = lax.axis_index("tm")
    return place < 2, lax.rem(place, 2) == 1


def slice_kernel(pix_hbm, out_ref, sem):
    copy = pltpu.make_async_copy(pix_hbm.at[pix_hbm.shape[0] - 1], out_ref, sem)
    copy.start()
    copy.wait()


def front_kernel(pix_hbm, we_hbm, gain_hbm, wk_hbm, wv_hbm, wq_hbm, wo_hbm,
                 emb, nor, key_most, key_rest, we, gain_ref, wk, wv, wq, wo, pix, we_sem, sem, late_sem):
    rows, width = emb.shape
    tub = key_most.shape[0] + 1
    pat = rows // tub
    size, cut = rows // 2, width // 5 * 2
    parts = [slice(i * size, (i + 1) * size) for i in range(2)]
    halves = [slice(0, cut), slice(cut, width)]
    loads = copy_in(
        [
            (pix_hbm.at[pl.ds(0, size)], pix.at[pl.ds(0, size)]),
            (we_hbm.at[:, pl.ds(0, cut)], we.at[:, pl.ds(0, cut)]),
            (pix_hbm.at[pl.ds(size, size)], pix.at[pl.ds(size, size)]),
            (we_hbm.at[:, pl.ds(cut, width - cut)], we.at[:, pl.ds(cut, width - cut)]),
        ],
        we_sem,
    )
    more = copy_in([(gain_hbm, gain_ref), (wk_hbm, wk)], sem)
    for j, half in enumerate(halves):
        for i, part in enumerate(parts):
            if j == 0:
                loads[2 * i].wait()
            if i == 0:
                loads[1 + 2 * j].wait()
            if i == j == 1:
                later = copy_in([(wv_hbm, wv), (wq_hbm, wq), (wo_hbm, wo)], late_sem)
            emb[part, half] = jnp.dot(
                pix[part, :], we[:, half], preferred_element_type=F32
            ).astype(BF)
    more[0].wait()
    gain = gain_ref[...].reshape(1, width)
    for t in range(tub):
        part = slice(t * pat, (t + 1) * pat)
        nor[part, :] = normed_rows(emb, part, gain)
    more[1].wait()
    for i, part in enumerate(parts):
        product = jnp.dot(nor[part, :], wk[...], preferred_element_type=F32).astype(BF)
        for u in range(size // pat):
            t = i * (size // pat) + u
            turned = product[u * pat:(u + 1) * pat, :].T
            if t < tub - 1:
                key_most[t] = turned
            else:
                key_rest[0] = turned
    for load in later:
        load.wait()


def tubelets(refs):
    return [ref.at[t] for ref in refs for t in range(ref.shape[0])]


def second_kernel(nor, wv, wq, value_most, query, *values):
    tub, _, pat = query.shape
    size = nor.shape[0] // 2
    for weight, target in ((wv, tubelets(values)), (wq, tubelets([query]))):
        for i in range(2):
            product = jnp.dot(
                nor[i * size:(i + 1) * size, :], weight[...], preferred_element_type=F32
            ).astype(BF)
            for u in range(size // pat):
                t = i * (size // pat) + u
                turned = product[u * pat:(u + 1) * pat, :].T
                target[t][...] = turned
                if weight is wv and t < tub - 1:
                    value_most[t] = turned


def ahead_kernel(pix, prior_hbm, we, gain_ref, wk, wv, out, value_last, emb, held, sem):
    tub = out.shape[1] // 2
    pat = out.shape[3]
    first, second = position()

    @pl.when(first)
    def _():
        copies = copy_in([(prior_hbm.at[i], held.at[i]) for i in range(2)], sem)
        for i in range(2):
            copies[i].wait()
            for t in range(2 * tub):
                there = (t + second.astype(jnp.int32) * tub) % (2 * tub)
                out[i, t] = held[i, there].T

    @pl.when(jnp.logical_not(first))
    def _():
        emb[...] = jnp.dot(pix[...], we[...], preferred_element_type=F32).astype(BF)
        gain = gain_ref[...].reshape(1, emb.shape[1])
        nor = normed_rows(emb, slice(0, pat), gain)
        for i, weight in enumerate((wk, wv)):
            turned = jnp.dot(nor, weight[...], preferred_element_type=F32).astype(BF).T
            out[i, tub - 1] = turned
            if i == 1:
                value_last[0] = turned


def pack_key_kernel(most_ref, rest_ref, sent_ref, ahead_ref, *outs):
    tub = most_ref.shape[0] + 1
    size = tub // len(outs)
    _, second = position()
    for t in range(tub):
        out = outs[t // size].at[t % size]

        @pl.when(jnp.logical_not(second))
        def _():
            out[...] = most_ref[t] if t < tub - 1 else rest_ref[0]

        @pl.when(second)
        def _():
            out[...] = sent_ref[t] if t < tub - 1 else ahead_ref[0, t]


def pack_value_kernel(most_ref, *refs):
    *swapped_refs, out_ref = refs
    tub, half, _ = out_ref.shape
    _, second = position()

    @pl.when(jnp.logical_not(second))
    def _():
        for t, ref in enumerate(tubelets(swapped_refs)[:tub]):
            out_ref[t] = ref[0:half, :]

    @pl.when(second)
    def _():
        out_ref[...] = most_ref[:, half:, :]


def score_kernel(pieces, q_ref, sent_ref, ahead_ref, *refs):
    near_refs = refs[:pieces]
    most_ref, rest_ref, w_ref, s_ref, far_ref, near_ref = refs[pieces:]
    tub = q_ref.shape[0]
    reach = 2 * tub
    first, second = position()
    far_ref[tub - 1] = ahead_ref[0, tub - 1]

    @pl.when(first)
    def _():
        far_ref[0:tub - 1] = ahead_ref[0, 0:tub - 1]

    @pl.when(jnp.logical_not(first))
    def _():
        far_ref[0:tub - 1] = sent_ref[...]

    @pl.when(first & jnp.logical_not(second))
    def _():
        near_ref[...] = ahead_ref[0, tub:]

    @pl.when(jnp.logical_not(first) | second)
    def _():
        for t in range(tub):
            near_ref[t] = tubelets(near_refs)[t][...]

    keys = tubelets((far_ref, near_ref, most_ref, rest_ref))

    def head(h, carry):
        part = head_rows(h)
        queries = [q_ref[t, part, :].astype(F32) for t in range(tub)]
        for j in range(3 * tub):
            key = keys[j][part, :].astype(F32)
            for t in range(max(0, j - reach), min(j, tub - 1) + 1):
                s_ref[t, j - t, pl.ds(h, 1), :] = jnp.sum(queries[t] * key, axis=0, keepdims=True)
        return carry

    lax.fori_loop(0, HEADS, head, 0)
    scale = 1.0 / math.sqrt(HEAD_DIM)
    for t in range(tub):
        scores = [s_ref[t, j] * scale for j in range(reach + 1)]
        top = functools.reduce(jnp.maximum, scores)
        expo = [jnp.exp(s - top) for s in scores]
        total = functools.reduce(jnp.add, expo)
        for j in range(reach + 1):
            w_ref[t, j] = (expo[j] / total).astype(BF).astype(F32)


def mix_kernel(pieces, w_ref, ahead_ref, held_ref, other_ref, last_ref, e_ref, wo_ref, *refs):
    swapped, own = tubelets(refs[:pieces]), tubelets(refs[pieces:2 * pieces])
    out_hbm, acc_ref, odd_ref, near_ref, mix, out_vmem, sem = refs[2 * pieces:]
    tub = len(own)
    reach = 2 * tub
    half = held_ref.shape[1]
    first, second = position()

    @pl.when(second)
    def _():
        odd_ref[:, 0:half, :] = other_ref[...]
        odd_ref[:, half:, :] = held_ref[...]
        for t in range(tub):
            near_ref[t] = swapped[t][...]

    @pl.when(jnp.logical_not(second) & jnp.logical_not(first))
    def _():
        near_ref[0:tub - 1, 0:half, :] = held_ref[...]
        near_ref[0:tub - 1, half:, :] = other_ref[...]
        near_ref[tub - 1] = last_ref[0]

    @pl.when(jnp.logical_not(second) & first)
    def _():
        near_ref[...] = ahead_ref[1, tub:]

    values = [ahead_ref.at[1, tub - 1], *tubelets([near_ref]), *own]

    def head(h, carry):
        part = head_rows(h)
        sums = [None] * tub
        for j in range(tub - 1, 3 * tub):
            value = values[j - tub + 1][part, :].astype(F32)
            for t in range(max(0, j - reach), min(j, tub - 1) + 1):
                term = w_ref[t, j - t, pl.ds(h, 1), :] * value
                sums[t] = term if sums[t] is None else sums[t] + term
        for t in range(tub - 1):
            acc_ref[t, part, :] = sums[t]
        mix[part, :] = sums[tub - 1].astype(BF)
        return carry

    lax.fori_loop(0, HEADS, head, 0)
    finish_rows(mix[...], e_ref.at[tub - 1], wo_ref, out_vmem, out_hbm.at[tub - 1], sem).wait()


def finish_rows(mixed, e_ref, wo_ref, out_vmem, out_hbm, sem):
    product = jnp.dot(mixed.T, wo_ref[...], preferred_element_type=F32)
    out_vmem[...] = (e_ref[...].astype(F32) + product).astype(BF)
    store = pltpu.make_async_copy(out_vmem, out_hbm, sem)
    store.start()
    return store


def finish_kernel(w_ref, odd_ref, even_ref, ahead_ref, acc_ref, e_ref, wo_ref, _, out_hbm, far, out_vmem, sem):
    count = far.shape[0]
    first, second = position()

    @pl.when(first)
    def _():
        far[...] = ahead_ref[1, 0:count]

    @pl.when(jnp.logical_not(first) & second)
    def _():
        far[...] = odd_ref[...]

    @pl.when(jnp.logical_not(first) & jnp.logical_not(second))
    def _():
        far[...] = even_ref[...]

    stores = []
    for t in reversed(range(count)):
        heads = []
        for h in range(HEADS):
            part = slice(h * HEAD_DIM, (h + 1) * HEAD_DIM)
            total = acc_ref[t, part, :]
            for j in range(t, count):
                total = total + w_ref[t, j - t, h:h + 1, :] * far[j, part, :].astype(F32)
            heads.append(total.astype(BF))
        mixed = jnp.concatenate(heads, axis=0)
        stores.append(
            finish_rows(mixed, e_ref.at[t], wo_ref, out_vmem.at[t], out_hbm.at[t], sem.at[t])
        )
    for store in stores:
        store.wait()


def body(pixels, prior_kv, w_embed, ln_gain, w_query, w_key, w_value, w_out):
    tub, pat, pix = pixels.shape
    width, inner = w_query.shape
    rows, reach = tub * pat, 2 * tub
    count = lax.axis_size("tm")
    turned = (tub, inner, pat)
    most, rest = (tub - 1, inner, pat), (1, inner, pat)
    dma = pltpu.SemaphoreType.DMA

    def in_hbm(value):
        return pltpu.with_memory_space_constraint(value, pltpu.HBM)

    def ring(value):
        return lax.ppermute(value, "tm", [(i, (i + 2) % count) for i in range(count)])

    def shift(value, start=0, step=1):
        return lax.ppermute(value, "tm", [(i, i + 2) for i in range(start, count - 2, step)])

    def swap(value):
        return lax.ppermute(value, "tm", [(i, i ^ 1) for i in range(count)])

    pix_ahead = ring(
        call(
            slice_kernel, "slice", 16, shape((pat, pix)), [HBM], VMEM, [dma]
        )(in_hbm(pixels))
    )
    embedded, normed, key_most, key_rest, w_embed, ln_gain, w_key, w_value, w_query, w_out = call(
        front_kernel, "front", 24,
        (
            shape((rows, width)), shape((rows, width)), shape(most), shape(rest),
            shape(w_embed.shape), shape(ln_gain.shape, F32), shape(w_key.shape),
            shape(w_value.shape), shape(w_query.shape), shape(w_out.shape),
        ),
        [HBM] * 7, (VMEM,) * 10,
        [pltpu.VMEM((rows, pix), BF), dma((4,)), dma((2,)), dma((3,))],
    )(
        in_hbm(pixels.reshape(rows, pix)), in_hbm(w_embed), in_hbm(ln_gain),
        in_hbm(w_key), in_hbm(w_value), in_hbm(w_query), in_hbm(w_out),
    )
    key_sent = ring(key_most)
    value_most, query, *value = call(
        second_kernel, "second", 16,
        (shape(most), shape(turned), *[shape((tub // V_PIECES, inner, pat))] * V_PIECES),
        [VMEM] * 3, (VMEM,) * (2 + V_PIECES),
    )(normed, w_value, w_query)
    value_swapped = [swap(part) for part in value]
    value_half = shift(
        call(
            pack_value_kernel, "pack_value", 16,
            shape((tub - 1, inner // 2, pat)), [VMEM] * (1 + V_PIECES), VMEM,
        )(value_most, *value_swapped)
    )
    value_even = shift(value_most, 0, 2)
    ahead, value_last = call(
        ahead_kernel, "ahead", 24,
        (shape((2, reach, inner, pat)), shape(rest)),
        [VMEM, HBM, VMEM, VMEM, VMEM, VMEM], (VMEM,) * 2,
        [pltpu.VMEM((pat, width), BF), pltpu.VMEM((2, reach, pat, inner), BF), dma((2,))],
    )(pix_ahead, in_hbm(prior_kv), w_embed, ln_gain, w_key, w_value)
    key_near = [
        swap(part)
        for part in call(
            pack_key_kernel, "pack_key", 16,
            (shape((tub // K_PIECES, inner, pat)),) * K_PIECES,
            [VMEM] * 4, (VMEM,) * K_PIECES,
        )(key_most, key_rest, key_sent, ahead)
    ]
    value_last = swap(value_last)
    weights = call(
        functools.partial(score_kernel, K_PIECES), "score", 16,
        shape((tub, reach + 1, HEADS, pat), F32),
        [VMEM] * (5 + K_PIECES), VMEM,
        [
            pltpu.VMEM((tub, reach + 1, HEADS, pat), F32), pltpu.VMEM(turned, BF),
            pltpu.VMEM(turned, BF),
        ],
    )(query, key_sent, ahead, *key_near, key_most, key_rest)
    value_other = swap(value_half)
    embedded = embedded.reshape(tub, pat, width)
    out, left, odd = call(
        functools.partial(mix_kernel, V_PIECES), "mix", 24,
        (shape((tub, pat, width)), shape(most, F32), shape(most)),
        [VMEM] * (7 + 2 * V_PIECES), (ANY, VMEM, VMEM),
        [pltpu.VMEM(turned, BF), pltpu.VMEM((inner, pat), BF), pltpu.VMEM((pat, width), BF), dma],
    )(weights, ahead, value_half, value_other, value_last, embedded, w_out, *value_swapped, *value)
    return call(
        finish_kernel, "finish", 24,
        shape((tub, pat, width)),
        [VMEM] * 7 + [ANY], ANY,
        [
            pltpu.VMEM(most, BF), pltpu.VMEM((tub - 1, pat, width), BF), dma((tub - 1,)),
        ],
        {7: 0},
    )(weights, odd, value_even, ahead, left, embedded, w_out, out)


def solution(mesh):
    placed = (
        P(("groups", "tm"), None, None),
        P(None, "groups", None, None),
        P(),
        P(),
        P(),
        P(),
        P(),
        P(),
    )
    return jax.shard_map(
        body, mesh=mesh, in_specs=placed, out_specs=P(("groups", "tm"), None, None), check_vma=False
    )
```

profile of v0, /device:TPU:10, one launch (start us, length us, event | category | flops | bytes accessed | tf_op | source)
XLA Modules:
  0.0 35.8 jit_solution(3487916470033479318)
XLA Ops:
  0.0 1.0 %slice.1 = bf16[128,1536]{1,0:T(8,128)(2,1)S(1)} custom-call(bf16[4,128,1536]{2,1,0:T(8,128)(2,1)} %pix_hbm.1), custom_call_target="tpu_custom_call" | custom-call | flops 1000000 | bytes 1 | tf_op jit(solution)/shard_map/slice/pallas_call | solution.py:359
  1.0 1.6 %collective-permute-start.1 = (bf16[128,1536]{1,0:T(8,128)(2,1)S(1)}, bf16[128,1536]{1,0:T(8,128)(2,1)S(1)}, u32[]{:S(2)}, u32[]{:S(2)}) collective-permute-start(bf16[128,1536]{1,0:T(8,128)(2,1)S(1)} %slice.1), channel_id=1, source_target_pairs={{0,2},{1,3},{2,4},{3,5},{4,6},{5,7},{6,8},{7,9},{8,10},{9,11},{10,... | collective-permute-start | bytes 1179656 | tf_op jit(solution)/shard_map/ppermute | solution.py:350
  2.6 6.4 %front.1 = (bf16[512,1280]{1,0:T(8,128)(2,1)S(1)}, bf16[512,1280]{1,0:T(8,128)(2,1)S(1)}, bf16[3,640,128]{2,1,0:T(8,128)(2,1)S(1)}, bf16[1,640,128]{2,1,0:T(8,12...) custom-call(bf16[512,1536]{1,0:T(8,128)(2,1)} %bitcast.4, ...), custom_call_target="tpu_custom_call" | custom-call | flops 36999999488 | bytes 1 | tf_op jit(solution)/shard_map/front/pallas_call | solution.py:363
  9.0 1.6 %collective-permute-start = (bf16[3,640,128]{2,1,0:T(8,128)(2,1)S(1)}, bf16[3,640,128]{2,1,0:T(8,128)(2,1)S(1)}, u32[]{:S(2)}, u32[]{:S(2)}) collective-permute-start(bf16[3,640,128]{2,1,0:T(8,128)(2,1)S(1)} %get-tuple-element.30.most_ref.refs_2_), channel_id=1, source_target_pairs={{0,2},{1,3},{2,4},{3,5},{4,6},{5,7},{6,8},{7,9},{8,10},{9,11},{10,... | collective-permute-start | bytes 1474568 | tf_op jit(solution)/shard_map/ppermute | solution.py:350
  10.5 2.3 %second.1 = (bf16[3,640,128]{2,1,0:T(8,128)(2,1)S(1)}, bf16[4,640,128]{2,1,0:T(8,128)(2,1)S(1)}, bf16[2,640,128]{2,1,0:T(8,128)(2,1)S(1)}, bf16[2,640,128]{2,1,0:T(8,128)(2,1)S(1)}) custom-call(bf16[512,1280]{1,0:T(8,128)(2,1)S(1)} %get-tuple-element.26.nor, bf16[1280,640]{1,0:T(8,128)(2,1)S(1)} %get-tuple-element.27.wv, ...), custom_call_target="tpu_custom_call" | custom-call | flops 1000000 | bytes 1 | tf_op jit(solution)/shard_map/second/pallas_call | solution.py:377
  12.8 0.1 collective-permute-start.4
  12.9 0.5 %collective-permute-start.5 = (bf16[2,640,128]{2,1,0:T(8,128)(2,1)S(1)}, bf16[2,640,128]{2,1,0:T(8,128)(2,1)S(1)}, u32[]{:S(2)}, u32[]{:S(2)}) collective-permute-start(bf16[2,640,128]{2,1,0:T(8,128)(2,1)S(1)} %get-tuple-element.40.refs_3_), channel_id=1, source_target_pairs={{0,1},{1,0},{2,3},{3,2},{4,5},{5,4},{6,7},{7,6},{8,9},{9,8},{10,11... | collective-permute-start | bytes 983048 | tf_op jit(solution)/shard_map/ppermute | solution.py:356
  13.4 1.1 %collective-permute-done.4.refs_0_ = bf16[2,640,128]{2,1,0:T(8,128)(2,1)S(1)} collective-permute-done((bf16[2,640,128]{2,1,0:T(8,128)(2,1)S(1)}, bf16[2,640,128]{2,1,0:T(8,128)(2,1)S(1)}, u32[]{:S(2)}, u32[]{:S(2)}) %collective-permute-start.4) | collective-permute-done | bytes 327712 | tf_op jit(solution)/shard_map/ppermute | solution.py:356
  14.5 0.5 %collective-permute-done.5.refs_1_ = bf16[2,640,128]{2,1,0:T(8,128)(2,1)S(1)} collective-permute-done((bf16[2,640,128]{2,1,0:T(8,128)(2,1)S(1)}, bf16[2,640,128]{2,1,0:T(8,128)(2,1)S(1)}, u32[]{:S(2)}, u32[]{:S(2)}) %collective-permute-start.5) | collective-permute-done | bytes 327712 | tf_op jit(solution)/shard_map/ppermute | solution.py:356
  15.0 3.4 %collective-permute-start.6 = (bf16[3,320,128]{2,1,0:T(8,128)(2,1)S(1)}, bf16[3,320,128]{2,1,0:T(8,128)(2,1)S(1)}, u32[]{:S(2)}, u32[]{:S(2)}) collective-permute-start(bf16[3,320,128]{2,1,0:T(8,128)(2,1)S(1)} %pack_value.1), channel_id=1, source_target_pairs={{0,2},{1,3},{2,4},{3,5},{4,6},{5,7},{6,8},{7,9},{8,10},{9,11},{10,... | collective-permute-start | bytes 737288 | tf_op jit(solution)/shard_map/ppermute | solution.py:353
  18.5 3.4 %collective-permute-start.9 = (bf16[3,640,128]{2,1,0:T(8,128)(2,1)S(1)}, bf16[3,640,128]{2,1,0:T(8,128)(2,1)S(1)}, u32[]{:S(2)}, u32[]{:S(2)}) collective-permute-start(bf16[3,640,128]{2,1,0:T(8,128)(2,1)S(1)} %get-tuple-element.38.most_ref), channel_id=1, source_target_pairs={{0,2},{2,4},{4,6},{6,8},{8,10},{10,12},{12,14},{16,18},{18,20},{20... | collective-permute-start | bytes 1474568 | tf_op jit(solution)/shard_map/ppermute | solution.py:353
  21.9 0.0 collective-permute-done.1.pix
  21.9 1.8 %ahead.1 = (bf16[2,8,640,128]{3,2,1,0:T(8,128)(2,1)S(1)}, bf16[1,640,128]{2,1,0:T(8,128)(2,1)S(1)}) custom-call(bf16[128,1536]{1,0:T(8,128)(2,1)S(1)} %collective-permute-done.1.pix, bf16[2,8,128,640]{3,2,1,0:T(8,128)(2,1)} %prior_hbm.1, bf16[1536,1280]{1,0:T(8,128)(2,1)S(1)} %get-tuple-element.31.we, f32[1280]{0:T(1024)S(1)} %get-tuple-element.32.gain_ref, ...), custom_call_target="tpu_custom_call" | custom-call | flops 1300000000 | bytes 1 | tf_op jit(solution)/shard_map/ahead/pallas_call | solution.py:390
  23.7 0.3 collective-permute-done.sent_ref
  24.1 0.1 collective-permute-start.2
  24.2 0.5 %collective-permute-start.3 = (bf16[2,640,128]{2,1,0:T(8,128)(2,1)S(1)}, bf16[2,640,128]{2,1,0:T(8,128)(2,1)S(1)}, u32[]{:S(2)}, u32[]{:S(2)}) collective-permute-start(bf16[2,640,128]{2,1,0:T(8,128)(2,1)S(1)} %get-tuple-element.37), channel_id=1, source_target_pairs={{0,1},{1,0},{2,3},{3,2},{4,5},{5,4},{6,7},{7,6},{8,9},{9,8},{10,11... | collective-permute-start | bytes 983048 | tf_op jit(solution)/shard_map/ppermute | solution.py:356
  24.7 3.9 %collective-permute-done.6.held_ref = bf16[3,320,128]{2,1,0:T(8,128)(2,1)S(1)} collective-permute-done((bf16[3,320,128]{2,1,0:T(8,128)(2,1)S(1)}, bf16[3,320,128]{2,1,0:T(8,128)(2,1)S(1)}, u32[]{:S(2)}, u32[]{:S(2)}) %collective-permute-start.6) | collective-permute-done | bytes 245792 | tf_op jit(solution)/shard_map/ppermute | solution.py:353
  28.6 0.0 collective-permute-start.7
  28.6 0.5 %collective-permute-start.8 = (bf16[1,640,128]{2,1,0:T(8,128)(2,1)S(1)}, bf16[1,640,128]{2,1,0:T(8,128)(2,1)S(1)}, u32[]{:S(2)}, u32[]{:S(2)}) collective-permute-start(bf16[1,640,128]{2,1,0:T(8,128)(2,1)S(1)} %get-tuple-element.41), channel_id=1, source_target_pairs={{0,1},{1,0},{2,3},{3,2},{4,5},{5,4},{6,7},{7,6},{8,9},{9,8},{10,11... | collective-permute-start | bytes 491528 | tf_op jit(solution)/shard_map/ppermute | solution.py:356
  29.1 0.0 collective-permute-done.2.refs_0_
  29.1 0.0 collective-permute-done.3.refs_1_
  29.1 1.4 %score.1.w_ref = f32[4,9,8,128]{3,2,1,0:T(8,128)S(1)} custom-call(bf16[4,640,128]{2,1,0:T(8,128)(2,1)S(1)} %get-tuple-element.29.q_ref, bf16[3,640,128]{2,1,0:T(8,128)(2,1)S(1)} %collective-permute-done.sent_ref, bf16[2,8,640,128]{3,2,1,0:T(8,128)(2,1)S(1)} %get-tuple-element.34.ahead_ref, bf16[2,640,128]{2,1,0:T(8,128)(2,1)S(1)} %collective-permute-done.2.refs_0_, ...), custom_call_target="tpu_custom_call" | custom-call | flops 1000000 | bytes 1 | tf_op jit(solution)/shard_map/score/pallas_call | solution.py:405
  30.5 0.0 collective-permute-done.8.last_ref
  30.5 0.0 collective-permute-done.7.other_ref
  30.5 2.0 %mix.1 = (bf16[4,128,1280]{2,1,0:T(8,128)(2,1)}, f32[3,640,128]{2,1,0:T(8,128)S(1)}, bf16[3,640,128]{2,1,0:T(8,128)(2,1)S(1)}) custom-call(f32[4,9,8,128]{3,2,1,0:T(8,128)S(1)} %score.1.w_ref, bf16[2,8,640,128]{3,2,1,0:T(8,128)(2,1)S(1)} %get-tuple-element.34.ahead_ref, bf16[3,320,128]{2,1,0:T(8,128)(2,1)S(1)} %collective-permute-done.6.held_ref, ...), custom_call_target="tpu_custom_call" | custom-call | flops 1000000 | bytes 1 | tf_op jit(solution)/shard_map/mix/pallas_call | solution.py:416
  32.6 1.3 %collective-permute-done.9.even_ref = bf16[3,640,128]{2,1,0:T(8,128)(2,1)S(1)} collective-permute-done((bf16[3,640,128]{2,1,0:T(8,128)(2,1)S(1)}, bf16[3,640,128]{2,1,0:T(8,128)(2,1)S(1)}, u32[]{:S(2)}, u32[]{:S(2)}) %collective-permute-start.9) | collective-permute-done | bytes 491552 | tf_op jit(solution)/shard_map/ppermute | solution.py:353
  33.9 1.9 %finish.1 = bf16[4,128,1280]{2,1,0:T(8,128)(2,1)} custom-call(f32[4,9,8,128]{3,2,1,0:T(8,128)S(1)} %score.1.w_ref, bf16[3,640,128]{2,1,0:T(8,128)(2,1)S(1)} %get-tuple-element.44.odd_ref, bf16[3,640,128]{2,1,0:T(8,128)(2,1)S(1)} %collective-permute-done.9.even_ref, ...), custom_call_target="tpu_custom_call", output_to_operand_aliasing={{}: (7, {})} | custom-call | flops 1000000 | bytes 1 | tf_op jit(solution)/shard_map/finish/pallas_call | solution.py:422
  (2 shorter events, 0.1 us)
Async XLA Ops:
  1.0 20.9 %collective-permute-start.1 = (bf16[128,1536]{1,0:T(8,128)(2,1)S(1)}, bf16[128,1536]{1,0:T(8,128)(2,1)S(1)}, u32[]{:S(2)}, u32[]{:S(2)}) collective-permute-start(bf16[128,1536]{1,0:T(8,128)(2,1)S(1)} %slice.1), channel_id=1, source_target_pairs={{0,2},{1,3},{2,4},{3,5},{4,6},{5,7},{6,8},{7,9},{8,10},{9,11},{10,... | collective-permute-start | bytes 1179656 | tf_op jit(solution)/shard_map/ppermute | solution.py:350
  9.0 15.1 %collective-permute-start = (bf16[3,640,128]{2,1,0:T(8,128)(2,1)S(1)}, bf16[3,640,128]{2,1,0:T(8,128)(2,1)S(1)}, u32[]{:S(2)}, u32[]{:S(2)}) collective-permute-start(bf16[3,640,128]{2,1,0:T(8,128)(2,1)S(1)} %get-tuple-element.30.most_ref.refs_2_), channel_id=1, source_target_pairs={{0,2},{1,3},{2,4},{3,5},{4,6},{5,7},{6,8},{7,9},{8,10},{9,11},{10,... | collective-permute-start | bytes 1474568 | tf_op jit(solution)/shard_map/ppermute | solution.py:350
  12.8 1.7 %collective-permute-start.4 = (bf16[2,640,128]{2,1,0:T(8,128)(2,1)S(1)}, bf16[2,640,128]{2,1,0:T(8,128)(2,1)S(1)}, u32[]{:S(2)}, u32[]{:S(2)}) collective-permute-start(bf16[2,640,128]{2,1,0:T(8,128)(2,1)S(1)} %get-tuple-element.39.refs_2_), channel_id=1, source_target_pairs={{0,1},{1,0},{2,3},{3,2},{4,5},{5,4},{6,7},{7,6},{8,9},{9,8},{10,11... | collective-permute-start | bytes 983048 | tf_op jit(solution)/shard_map/ppermute | solution.py:356
  12.9 2.1 %collective-permute-start.5 = (bf16[2,640,128]{2,1,0:T(8,128)(2,1)S(1)}, bf16[2,640,128]{2,1,0:T(8,128)(2,1)S(1)}, u32[]{:S(2)}, u32[]{:S(2)}) collective-permute-start(bf16[2,640,128]{2,1,0:T(8,128)(2,1)S(1)} %get-tuple-element.40.refs_3_), channel_id=1, source_target_pairs={{0,1},{1,0},{2,3},{3,2},{4,5},{5,4},{6,7},{7,6},{8,9},{9,8},{10,11... | collective-permute-start | bytes 983048 | tf_op jit(solution)/shard_map/ppermute | solution.py:356
  15.0 13.6 %collective-permute-start.6 = (bf16[3,320,128]{2,1,0:T(8,128)(2,1)S(1)}, bf16[3,320,128]{2,1,0:T(8,128)(2,1)S(1)}, u32[]{:S(2)}, u32[]{:S(2)}) collective-permute-start(bf16[3,320,128]{2,1,0:T(8,128)(2,1)S(1)} %pack_value.1), channel_id=1, source_target_pairs={{0,2},{1,3},{2,4},{3,5},{4,6},{5,7},{6,8},{7,9},{8,10},{9,11},{10,... | collective-permute-start | bytes 737288 | tf_op jit(solution)/shard_map/ppermute | solution.py:353
  18.5 15.4 %collective-permute-start.9 = (bf16[3,640,128]{2,1,0:T(8,128)(2,1)S(1)}, bf16[3,640,128]{2,1,0:T(8,128)(2,1)S(1)}, u32[]{:S(2)}, u32[]{:S(2)}) collective-permute-start(bf16[3,640,128]{2,1,0:T(8,128)(2,1)S(1)} %get-tuple-element.38.most_ref), channel_id=1, source_target_pairs={{0,2},{2,4},{4,6},{6,8},{8,10},{10,12},{12,14},{16,18},{18,20},{20... | collective-permute-start | bytes 1474568 | tf_op jit(solution)/shard_map/ppermute | solution.py:353
  24.1 5.0 %collective-permute-start.2 = (bf16[2,640,128]{2,1,0:T(8,128)(2,1)S(1)}, bf16[2,640,128]{2,1,0:T(8,128)(2,1)S(1)}, u32[]{:S(2)}, u32[]{:S(2)}) collective-permute-start(bf16[2,640,128]{2,1,0:T(8,128)(2,1)S(1)} %get-tuple-element.36), channel_id=1, source_target_pairs={{0,1},{1,0},{2,3},{3,2},{4,5},{5,4},{6,7},{7,6},{8,9},{9,8},{10,11... | collective-permute-start | bytes 983048 | tf_op jit(solution)/shard_map/ppermute | solution.py:356
  24.2 5.0 %collective-permute-start.3 = (bf16[2,640,128]{2,1,0:T(8,128)(2,1)S(1)}, bf16[2,640,128]{2,1,0:T(8,128)(2,1)S(1)}, u32[]{:S(2)}, u32[]{:S(2)}) collective-permute-start(bf16[2,640,128]{2,1,0:T(8,128)(2,1)S(1)} %get-tuple-element.37), channel_id=1, source_target_pairs={{0,1},{1,0},{2,3},{3,2},{4,5},{5,4},{6,7},{7,6},{8,9},{9,8},{10,11... | collective-permute-start | bytes 983048 | tf_op jit(solution)/shard_map/ppermute | solution.py:356
  28.6 1.9 %collective-permute-start.7 = (bf16[3,320,128]{2,1,0:T(8,128)(2,1)S(1)}, bf16[3,320,128]{2,1,0:T(8,128)(2,1)S(1)}, u32[]{:S(2)}, u32[]{:S(2)}) collective-permute-start(bf16[3,320,128]{2,1,0:T(8,128)(2,1)S(1)} %collective-permute-done.6.held_ref), channel_id=1, source_target_pairs={{0,1},{1,0},{2,3},{3,2},{4,5},{5,4},{6,7},{7,6},{8,9},{9,8},{10,11... | collective-permute-start | bytes 737288 | tf_op jit(solution)/shard_map/ppermute | solution.py:356
  28.6 1.9 %collective-permute-start.8 = (bf16[1,640,128]{2,1,0:T(8,128)(2,1)S(1)}, bf16[1,640,128]{2,1,0:T(8,128)(2,1)S(1)}, u32[]{:S(2)}, u32[]{:S(2)}) collective-permute-start(bf16[1,640,128]{2,1,0:T(8,128)(2,1)S(1)} %get-tuple-element.41), channel_id=1, source_target_pairs={{0,1},{1,0},{2,3},{3,2},{4,5},{5,4},{6,7},{7,6},{8,9},{9,8},{10,11... | collective-permute-start | bytes 491528 | tf_op jit(solution)/shard_map/ppermute | solution.py:356
where the time goes:
time: 36 us; the launch traced here: 35.8 us
  Pallas kernels  16.8 us (47%)
  starting transfers between devices  11.6 us (32%)
  waiting for transfers between devices  7.15 us (20%)
    ppermute x2, starting transfers between devices, shift(): lax.ppermute(value, 'tm', [(i, i + 2) for i in range(start, count - 2, st...  6.86 us
    pallas_call x1, Pallas kernels, body(): call(front_kernel, 'front', 24, (shape((rows, width)), shape((rows, width...  6.37 us
    ppermute x2, waiting for transfers between devices, shift(): lax.ppermute(value, 'tm', [(i, i + 2) for i in range(start, count - 2, st...  5.25 us
    ppermute x2, starting transfers between devices, ring(): lax.ppermute(value, 'tm', [(i, (i + 2) % count) for i in range(count)])  3.14 us
    pallas_call x1, Pallas kernels, body(): call(second_kernel, 'second', 16, (shape(most), shape(turned), *[shape((t...  2.29 us
    pallas_call x1, Pallas kernels, body(): call(functools.partial(mix_kernel, V_PIECES), 'mix', 24, (shape((tub, pat...  2.04 us
    pallas_call x1, Pallas kernels, body(): call(finish_kernel, 'finish', 24, shape((tub, pat, width)), [VMEM] * 7 +...  1.87 us
    pallas_call x1, Pallas kernels, body(): call(ahead_kernel, 'ahead', 24, (shape((2, reach, inner, pat)), shape(res...  1.84 us
  transfers between devices with their start and end apart: 10, of which 5 were waited for; matrix products, arithmetic and copies ran while one was open for 0% of the time, Pallas kernels for 39%

commit v1 on v0

--- a/solution.py
+++ b/solution.py
@@ -22,10 +22,11 @@
     return pltpu.CompilerParams(vmem_limit_bytes=mib * MIB)
 
 
-COST = {"slice": 1, "front": 37000, "second": 1, "ahead": 1300, "pack_key": 1, "pack_value": 1,
-        "score": 1, "mix": 1, "finish": 1}
+COST = {"slice": 1, "front": 37000, "second": 1, "ahead": 1300, "pack_key": 1000, "pack_value": 1,
+        "score": 1, "weight": 1, "mix": 1, "finish": 1}
 K_PIECES = 2
 V_PIECES = 2
+R_PIECES = 2
 
 
 def call(kernel, name, mib, out_shape, in_specs, out_specs, scratch=(), aliases=None):
@@ -129,7 +130,7 @@
     return [ref.at[t] for ref in refs for t in range(ref.shape[0])]
 
 
-def second_kernel(nor, wv, wq, value_most, query, *values):
+def second_kernel(nor, wv, wq, value_start, query, *values):
     tub, _, pat = query.shape
     size = nor.shape[0] // 2
     for weight, target in ((wv, tubelets(values)), (wq, tubelets([query]))):
@@ -141,8 +142,8 @@
                 t = i * (size // pat) + u
                 turned = product[u * pat:(u + 1) * pat, :].T
                 target[t][...] = turned
-                if weight is wv and t < tub - 1:
-                    value_most[t] = turned
+                if weight is wv and t < value_start.shape[0]:
+                    value_start[t] = turned
 
 
 def ahead_kernel(pix, prior_hbm, we, gain_ref, wk, wv, out, value_last, emb, held, sem):
@@ -187,36 +188,63 @@
             out[...] = sent_ref[t] if t < tub - 1 else ahead_ref[0, t]
 
 
-def pack_value_kernel(most_ref, *refs):
-    *swapped_refs, out_ref = refs
+def pack_value_kernel(pieces, *refs):
+    own, swapped, out_ref = tubelets(refs[:pieces]), tubelets(refs[pieces:2 * pieces]), refs[2 * pieces]
     tub, half, _ = out_ref.shape
     _, second = position()
 
     @pl.when(jnp.logical_not(second))
     def _():
-        for t, ref in enumerate(tubelets(swapped_refs)[:tub]):
-            out_ref[t] = ref[0:half, :]
+        for t in range(tub - 1):
+            out_ref[t] = swapped[t][0:half, :]
+        out_ref[tub - 1] = own[tub - 2][0:half, :]
 
     @pl.when(second)
     def _():
-        out_ref[...] = most_ref[:, half:, :]
-
-
-def score_kernel(pieces, q_ref, sent_ref, ahead_ref, *refs):
+        for t in range(tub - 1):
+            out_ref[t] = own[t][half:, :]
+        out_ref[tub - 1] = swapped[tub - 2][half:, :]
+
+
+def scored(blocks, q_ref, s_ref):
+    tub = q_ref.shape[0]
+    reach = 2 * tub
+
+    def head(h, carry):
+        part = head_rows(h)
+        queries = [q_ref[t, part, :].astype(F32) for t in range(tub)]
+        for j, key_ref in blocks.items():
+            key = key_ref[part, :].astype(F32)
+            for t in range(max(0, j - reach), min(j, tub - 1) + 1):
+                s_ref[t, j - t, pl.ds(h, 1), :] = jnp.sum(queries[t] * key, axis=0, keepdims=True)
+        return carry
+
+    lax.fori_loop(0, HEADS, head, 0)
+
+
+def score_kernel(q_ref, sent_ref, ahead_ref, most_ref, rest_ref, s_ref, far_ref):
+    tub = q_ref.shape[0]
+    first, _ = position()
+    far_ref[tub - 1] = ahead_ref[0, tub - 1]
+
+    @pl.when(first)
+    def _():
+        far_ref[0:tub - 1] = ahead_ref[0, 0:tub - 1]
+
+    @pl.when(jnp.logical_not(first))
+    def _():
+        far_ref[0:tub - 1] = sent_ref[...]
+
+    keys = tubelets([far_ref]) + [None] * tub + tubelets((most_ref, rest_ref))
+    scored({j: key for j, key in enumerate(keys) if key is not None}, q_ref, s_ref)
+
+
+def weight_kernel(pieces, q_ref, ahead_ref, far_own_ref, *refs):
     near_refs = refs[:pieces]
-    most_ref, rest_ref, w_ref, s_ref, far_ref, near_ref = refs[pieces:]
+    w_ref, s_ref, near_ref = refs[pieces:]
     tub = q_ref.shape[0]
     reach = 2 * tub
     first, second = position()
-    far_ref[tub - 1] = ahead_ref[0, tub - 1]
-
-    @pl.when(first)
-    def _():
-        far_ref[0:tub - 1] = ahead_ref[0, 0:tub - 1]
-
-    @pl.when(jnp.logical_not(first))
-    def _():
-        far_ref[0:tub - 1] = sent_ref[...]
 
     @pl.when(first & jnp.logical_not(second))
     def _():
@@ -227,83 +255,94 @@
         for t in range(tub):
             near_ref[t] = tubelets(near_refs)[t][...]
 
-    keys = tubelets((far_ref, near_ref, most_ref, rest_ref))
-
-    def head(h, carry):
-        part = head_rows(h)
-        queries = [q_ref[t, part, :].astype(F32) for t in range(tub)]
-        for j in range(3 * tub):
-            key = keys[j][part, :].astype(F32)
-            for t in range(max(0, j - reach), min(j, tub - 1) + 1):
-                s_ref[t, j - t, pl.ds(h, 1), :] = jnp.sum(queries[t] * key, axis=0, keepdims=True)
-        return carry
-
-    lax.fori_loop(0, HEADS, head, 0)
+    scored({tub + j: near_ref.at[j] for j in range(tub)}, q_ref, s_ref)
     scale = 1.0 / math.sqrt(HEAD_DIM)
     for t in range(tub):
-        scores = [s_ref[t, j] * scale for j in range(reach + 1)]
+        scores = [
+            (s_ref if tub <= t + d < reach else far_own_ref)[t, d] * scale for d in range(reach + 1)
+        ]
         top = functools.reduce(jnp.maximum, scores)
         expo = [jnp.exp(s - top) for s in scores]
         total = functools.reduce(jnp.add, expo)
-        for j in range(reach + 1):
-            w_ref[t, j] = (expo[j] / total).astype(BF).astype(F32)
-
-
-def mix_kernel(pieces, w_ref, ahead_ref, held_ref, other_ref, last_ref, e_ref, wo_ref, *refs):
+        for d in range(reach + 1):
+            w_ref[t, d] = (expo[d] / total).astype(BF).astype(F32)
+
+
+def mix_kernel(pieces, other_pieces, w_ref, ahead_ref, held_ref, last_ref, e_ref, wo_ref, *refs):
+    others, refs = refs[:other_pieces], refs[other_pieces:]
     swapped, own = tubelets(refs[:pieces]), tubelets(refs[pieces:2 * pieces])
-    out_hbm, acc_ref, odd_ref, near_ref, mix, out_vmem, sem = refs[2 * pieces:]
+    done_ref, acc_ref, odd_ref, near_ref, far_ref, mix = refs[2 * pieces:]
     tub = len(own)
-    reach = 2 * tub
+    reach, start = 2 * tub, acc_ref.shape[0]
     half = held_ref.shape[1]
     first, second = position()
 
+    def join(target, tubelet, low):
+        target[(slice(0, half) if low else slice(half, 2 * half)), :] = held_ref[tubelet]
+        for i, ref in enumerate(others):
+            size = ref.shape[1]
+            place = i * size + (half if low else 0)
+            target[place:place + size, :] = ref[tubelet]
+
     @pl.when(second)
     def _():
-        odd_ref[:, 0:half, :] = other_ref[...]
-        odd_ref[:, half:, :] = held_ref[...]
+        for t in range(start):
+            join(odd_ref.at[t], t, False)
         for t in range(tub):
             near_ref[t] = swapped[t][...]
 
+    @pl.when(second & jnp.logical_not(first))
+    def _():
+        join(far_ref, start, False)
+
     @pl.when(jnp.logical_not(second) & jnp.logical_not(first))
     def _():
-        near_ref[0:tub - 1, 0:half, :] = held_ref[...]
-        near_ref[0:tub - 1, half:, :] = other_ref[...]
+        for t in range(tub - 1):
+            join(near_ref.at[t], t, True)
         near_ref[tub - 1] = last_ref[0]
+        join(far_ref, tub - 1, True)
+
+    @pl.when(first)
+    def _():
+        far_ref[...] = ahead_ref[1, start]
 
     @pl.when(jnp.logical_not(second) & first)
     def _():
         near_ref[...] = ahead_ref[1, tub:]
 
-    values = [ahead_ref.at[1, tub - 1], *tubelets([near_ref]), *own]
+    values = [far_ref, ahead_ref.at[1, tub - 1], *tubelets([near_ref]), *own]
 
     def head(h, carry):
         part = head_rows(h)
         sums = [None] * tub
-        for j in range(tub - 1, 3 * tub):
-            value = values[j - tub + 1][part, :].astype(F32)
+        for j in range(start, 3 * tub):
+            value = values[j - start][part, :].astype(F32)
             for t in range(max(0, j - reach), min(j, tub - 1) + 1):
                 term = w_ref[t, j - t, pl.ds(h, 1), :] * value
                 sums[t] = term if sums[t] is None else sums[t] + term
-        for t in range(tub - 1):
-            acc_ref[t, part, :] = sums[t]
-        mix[part, :] = sums[tub - 1].astype(BF)
+        for t in range(tub):
+            if t < start:
+                acc_ref[t, part, :] = sums[t]
+            else:
+                mix[t - start, part, :] = sums[t].astype(BF)
         return carry
 
     lax.fori_loop(0, HEADS, head, 0)
-    finish_rows(mix[...], e_ref.at[tub - 1], wo_ref, out_vmem, out_hbm.at[tub - 1], sem).wait()
-
-
-def finish_rows(mixed, e_ref, wo_ref, out_vmem, out_hbm, sem):
+    for t in range(start, tub):
+        done_ref[t - start] = finished(mix[t - start], e_ref.at[t], wo_ref)
+
+
+def finished(mixed, e_ref, wo_ref):
     product = jnp.dot(mixed.T, wo_ref[...], preferred_element_type=F32)
-    out_vmem[...] = (e_ref[...].astype(F32) + product).astype(BF)
-    store = pltpu.make_async_copy(out_vmem, out_hbm, sem)
-    store.start()
-    return store
-
-
-def finish_kernel(w_ref, odd_ref, even_ref, ahead_ref, acc_ref, e_ref, wo_ref, _, out_hbm, far, out_vmem, sem):
+    return (e_ref[...].astype(F32) + product).astype(BF)
+
+
+def finish_kernel(w_ref, odd_ref, even_ref, ahead_ref, acc_ref, e_ref, wo_ref, done_ref,
+                  out_hbm, far, out_vmem, sem):
     count = far.shape[0]
     first, second = position()
+    written = pltpu.make_async_copy(done_ref, out_hbm.at[pl.ds(count, done_ref.shape[0])], sem.at[count])
+    written.start()
 
     @pl.when(first)
     def _():
@@ -317,7 +356,7 @@
     def _():
         far[...] = even_ref[...]
 
-    stores = []
+    stores = [written]
     for t in reversed(range(count)):
         heads = []
         for h in range(HEADS):
@@ -326,10 +365,9 @@
             for j in range(t, count):
                 total = total + w_ref[t, j - t, h:h + 1, :] * far[j, part, :].astype(F32)
             heads.append(total.astype(BF))
-        mixed = jnp.concatenate(heads, axis=0)
-        stores.append(
-            finish_rows(mixed, e_ref.at[t], wo_ref, out_vmem.at[t], out_hbm.at[t], sem.at[t])
-        )
+        out_vmem[t] = finished(jnp.concatenate(heads, axis=0), e_ref.at[t], wo_ref)
+        stores.append(pltpu.make_async_copy(out_vmem.at[t], out_hbm.at[t], sem.at[t]))
+        stores[-1].start()
     for store in stores:
         store.wait()
 
@@ -340,7 +378,7 @@
     rows, reach = tub * pat, 2 * tub
     count = lax.axis_size("tm")
     turned = (tub, inner, pat)
-    most, rest = (tub - 1, inner, pat), (1, inner, pat)
+    most, rest, start = (tub - 1, inner, pat), (1, inner, pat), (tub - 2, inner, pat)
     dma = pltpu.SemaphoreType.DMA
 
     def in_hbm(value):
@@ -374,25 +412,30 @@
         in_hbm(w_key), in_hbm(w_value), in_hbm(w_query), in_hbm(w_out),
     )
     key_sent = ring(key_most)
-    value_most, query, *value = call(
+    value_start, query, *value = call(
         second_kernel, "second", 16,
-        (shape(most), shape(turned), *[shape((tub // V_PIECES, inner, pat))] * V_PIECES),
+        (shape(start), shape(turned), *[shape((tub // V_PIECES, inner, pat))] * V_PIECES),
         [VMEM] * 3, (VMEM,) * (2 + V_PIECES),
     )(normed, w_value, w_query)
     value_swapped = [swap(part) for part in value]
     value_half = shift(
         call(
-            pack_value_kernel, "pack_value", 16,
-            shape((tub - 1, inner // 2, pat)), [VMEM] * (1 + V_PIECES), VMEM,
-        )(value_most, *value_swapped)
-    )
-    value_even = shift(value_most, 0, 2)
+            functools.partial(pack_value_kernel, V_PIECES), "pack_value", 16,
+            shape((tub, inner // 2, pat)), [VMEM] * (2 * V_PIECES), VMEM,
+        )(*value, *value_swapped)
+    )
+    value_even = shift(value_start, 0, 2)
     ahead, value_last = call(
         ahead_kernel, "ahead", 24,
         (shape((2, reach, inner, pat)), shape(rest)),
         [VMEM, HBM, VMEM, VMEM, VMEM, VMEM], (VMEM,) * 2,
         [pltpu.VMEM((pat, width), BF), pltpu.VMEM((2, reach, pat, inner), BF), dma((2,))],
     )(pix_ahead, in_hbm(prior_kv), w_embed, ln_gain, w_key, w_value)
+    scores = call(
+        score_kernel, "score", 16,
+        shape((tub, reach + 1, HEADS, pat), F32),
+        [VMEM] * 5, VMEM, [pltpu.VMEM(turned, BF)],
+    )(query, key_sent, ahead, key_most, key_rest)
     key_near = [
         swap(part)
         for part in call(
@@ -401,33 +444,31 @@
             [VMEM] * 4, (VMEM,) * K_PIECES,
         )(key_most, key_rest, key_sent, ahead)
     ]
+    value_last, scores = lax.optimization_barrier((value_last, scores))
     value_last = swap(value_last)
     weights = call(
-        functools.partial(score_kernel, K_PIECES), "score", 16,
+        functools.partial(weight_kernel, K_PIECES), "weight", 16,
         shape((tub, reach + 1, HEADS, pat), F32),
-        [VMEM] * (5 + K_PIECES), VMEM,
-        [
-            pltpu.VMEM((tub, reach + 1, HEADS, pat), F32), pltpu.VMEM(turned, BF),
-            pltpu.VMEM(turned, BF),
-        ],
-    )(query, key_sent, ahead, *key_near, key_most, key_rest)
-    value_other = swap(value_half)
+        [VMEM] * (3 + K_PIECES), VMEM,
+        [pltpu.VMEM((tub, reach + 1, HEADS, pat), F32), pltpu.VMEM(turned, BF)],
+    )(query, ahead, scores, *key_near)
+    cut = inner // 2 // R_PIECES
+    value_other = [swap(value_half[:, i * cut:(i + 1) * cut, :]) for i in range(R_PIECES)]
     embedded = embedded.reshape(tub, pat, width)
-    out, left, odd = call(
-        functools.partial(mix_kernel, V_PIECES), "mix", 24,
-        (shape((tub, pat, width)), shape(most, F32), shape(most)),
-        [VMEM] * (7 + 2 * V_PIECES), (ANY, VMEM, VMEM),
-        [pltpu.VMEM(turned, BF), pltpu.VMEM((inner, pat), BF), pltpu.VMEM((pat, width), BF), dma],
-    )(weights, ahead, value_half, value_other, value_last, embedded, w_out, *value_swapped, *value)
+    done, left, odd = call(
+        functools.partial(mix_kernel, V_PIECES, R_PIECES), "mix", 24,
+        (shape((2, pat, width)), shape(start, F32), shape(start)),
+        [VMEM] * (6 + R_PIECES + 2 * V_PIECES), (VMEM,) * 3,
+        [pltpu.VMEM(turned, BF), pltpu.VMEM((inner, pat), BF), pltpu.VMEM((2, inner, pat), BF)],
+    )(weights, ahead, value_half, value_last, embedded, w_out, *value_other, *value_swapped, *value)
     return call(
         finish_kernel, "finish", 24,
         shape((tub, pat, width)),
-        [VMEM] * 7 + [ANY], ANY,
+        [VMEM] * 8, ANY,
         [
-            pltpu.VMEM(most, BF), pltpu.VMEM((tub - 1, pat, width), BF), dma((tub - 1,)),
+            pltpu.VMEM(start, BF), pltpu.VMEM((tub - 2, pat, width), BF), dma((tub - 1,)),
         ],
-        {7: 0},
-    )(weights, odd, value_even, ahead, left, embedded, w_out, out)
+    )(weights, odd, value_even, ahead, left, embedded, w_out, done)
 
 
 def solution(mesh):

time: 36 us -> 36 us (level)
  waiting for transfers between devices: 7.15 us -> 8.33 us
  starting transfers between devices: 11.6 us -> 10.9 us
  Pallas kernels: 16.8 us -> 16.2 us
    ppermute x2, waiting for transfers between devices: 0.3 us -> 3.73 us  [ring(): lax.ppermute(value, 'tm', [(i, (i + 2) % count) for i in range(count)])]
    ppermute x2, waiting for transfers between devices: 5.25 us -> 2.6 us  [shift(): lax.ppermute(value, 'tm', [(i, i + 2) for i in range(start, count - 2, st...]
    ppermute x2, starting transfers between devices: 6.86 us -> 5.96 us  [shift(): lax.ppermute(value, 'tm', [(i, i + 2) for i in range(start, count - 2, st...]
    pallas_call x5 -> x6, Pallas kernels: 7.58 us -> 6.96 us  [the longest x1 2.29 us: body(): call(second_kernel, 'second', 16, (shape(start), shape(turned), *[shape((...]
    ppermute x6 -> x7, waiting for transfers between devices: 1.6 us -> 2 us  [swap(): return lax.ppermute(value, 'tm', [(i, i ^ 1) for i in range(count)])]
    ppermute x6 -> x7, starting transfers between devices: 1.65 us -> 1.77 us  [swap(): return lax.ppermute(value, 'tm', [(i, i ^ 1) for i in range(count)])]
  transfers between devices with their start and end apart: 10 -> 11, of which waited for: 5 -> 7; matrix products, arithmetic and copies ran while one was open for 0% -> 0% of each run, Pallas kernels for 39% -> 38%
where the time goes in v1:
time: 36 us; the launch traced here: 35.6 us
  Pallas kernels  16.2 us (45%)
  starting transfers between devices  10.9 us (30%)
  waiting for transfers between devices  8.33 us (23%)
    pallas_call x1, Pallas kernels, body(): call(front_kernel, 'front', 24, (shape((rows, width)), shape((rows, width...  6.37 us
    ppermute x2, starting transfers between devices, shift(): lax.ppermute(value, 'tm', [(i, i + 2) for i in range(start, count - 2, st...  5.96 us
    ppermute x2, waiting for transfers between devices, ring(): lax.ppermute(value, 'tm', [(i, (i + 2) % count) for i in range(count)])  3.73 us
    ppermute x2, starting transfers between devices, ring(): lax.ppermute(value, 'tm', [(i, (i + 2) % count) for i in range(count)])  3.14 us
    ppermute x2, waiting for transfers between devices, shift(): lax.ppermute(value, 'tm', [(i, i + 2) for i in range(start, count - 2, st...  2.6 us
    pallas_call x1, Pallas kernels, body(): call(second_kernel, 'second', 16, (shape(start), shape(turned), *[shape((...  2.29 us
    ppermute x7, waiting for transfers between devices, swap(): return lax.ppermute(value, 'tm', [(i, i ^ 1) for i in range(count)])  2 us
    pallas_call x1, Pallas kernels, body(): call(ahead_kernel, 'ahead', 24, (shape((2, reach, inner, pat)), shape(res...  1.84 us
  transfers between devices with their start and end apart: 11, of which 7 were waited for; matrix products, arithmetic and copies ran while one was open for 0% of the time, Pallas kernels for 38%

profile of v1, /device:TPU:10, one launch (start us, length us, event | category | flops | bytes accessed | tf_op | source)
XLA Modules:
  0.0 35.6 jit_solution(13596542458036608523)
XLA Ops:
  0.0 1.0 %slice.13 = bf16[128,1536]{1,0:T(8,128)(2,1)S(1)} custom-call(bf16[4,128,1536]{2,1,0:T(8,128)(2,1)} %pix_hbm.1), custom_call_target="tpu_custom_call" | custom-call | flops 1000000 | bytes 1 | tf_op jit(solution)/shard_map/slice/pallas_call | solution.py:397
  1.0 1.6 %collective-permute-start = (bf16[128,1536]{1,0:T(8,128)(2,1)S(1)}, bf16[128,1536]{1,0:T(8,128)(2,1)S(1)}, u32[]{:S(2)}, u32[]{:S(2)}) collective-permute-start(bf16[128,1536]{1,0:T(8,128)(2,1)S(1)} %slice.13), channel_id=1, source_target_pairs={{0,2},{1,3},{2,4},{3,5},{4,6},{5,7},{6,8},{7,9},{8,10},{9,11},{10,... | collective-permute-start | bytes 1179656 | tf_op jit(solution)/shard_map/ppermute | solution.py:388
  2.6 6.4 %front.1 = (bf16[512,1280]{1,0:T(8,128)(2,1)S(1)}, bf16[512,1280]{1,0:T(8,128)(2,1)S(1)}, bf16[3,640,128]{2,1,0:T(8,128)(2,1)S(1)}, bf16[1,640,128]{2,1,0:T(8,12...) custom-call(bf16[512,1536]{1,0:T(8,128)(2,1)} %bitcast.4, ...), custom_call_target="tpu_custom_call" | custom-call | flops 36999999488 | bytes 1 | tf_op jit(solution)/shard_map/front/pallas_call | solution.py:401
  9.0 1.6 %collective-permute-start.1 = (bf16[3,640,128]{2,1,0:T(8,128)(2,1)S(1)}, bf16[3,640,128]{2,1,0:T(8,128)(2,1)S(1)}, u32[]{:S(2)}, u32[]{:S(2)}) collective-permute-start(bf16[3,640,128]{2,1,0:T(8,128)(2,1)S(1)} %get-tuple-element.37.most_ref), channel_id=1, source_target_pairs={{0,2},{1,3},{2,4},{3,5},{4,6},{5,7},{6,8},{7,9},{8,10},{9,11},{10,... | collective-permute-start | bytes 1474568 | tf_op jit(solution)/shard_map/ppermute | solution.py:388
  10.5 2.3 %second.1 = (bf16[2,640,128]{2,1,0:T(8,128)(2,1)S(1)}, bf16[4,640,128]{2,1,0:T(8,128)(2,1)S(1)}, bf16[2,640,128]{2,1,0:T(8,128)(2,1)S(1)}, bf16[2,640,128]{2,1,0:T(8,128)(2,1)S(1)}) custom-call(bf16[512,1280]{1,0:T(8,128)(2,1)S(1)} %get-tuple-element.28.nor, bf16[1280,640]{1,0:T(8,128)(2,1)S(1)} %get-tuple-element.29.wv, ...), custom_call_target="tpu_custom_call" | custom-call | flops 1000000 | bytes 1 | tf_op jit(solution)/shard_map/second/pallas_call | solution.py:415
  12.8 0.1 collective-permute-start.4
  12.9 0.5 %collective-permute-start.5 = (bf16[2,640,128]{2,1,0:T(8,128)(2,1)S(1)}, bf16[2,640,128]{2,1,0:T(8,128)(2,1)S(1)}, u32[]{:S(2)}, u32[]{:S(2)}) collective-permute-start(bf16[2,640,128]{2,1,0:T(8,128)(2,1)S(1)} %get-tuple-element.43.refs_1_.refs_5_), channel_id=1, source_target_pairs={{0,1},{1,0},{2,3},{3,2},{4,5},{5,4},{6,7},{7,6},{8,9},{9,8},{10,11... | collective-permute-start | bytes 983048 | tf_op jit(solution)/shard_map/ppermute | solution.py:394
  13.4 1.1 %collective-permute-done.4.refs_2_ = bf16[2,640,128]{2,1,0:T(8,128)(2,1)S(1)} collective-permute-done((bf16[2,640,128]{2,1,0:T(8,128)(2,1)S(1)}, bf16[2,640,128]{2,1,0:T(8,128)(2,1)S(1)}, u32[]{:S(2)}, u32[]{:S(2)}) %collective-permute-start.4) | collective-permute-done | bytes 327712 | tf_op jit(solution)/shard_map/ppermute | solution.py:394
  14.5 0.5 %collective-permute-done.5.refs_3_ = bf16[2,640,128]{2,1,0:T(8,128)(2,1)S(1)} collective-permute-done((bf16[2,640,128]{2,1,0:T(8,128)(2,1)S(1)}, bf16[2,640,128]{2,1,0:T(8,128)(2,1)S(1)}, u32[]{:S(2)}, u32[]{:S(2)}) %collective-permute-start.5) | collective-permute-done | bytes 327712 | tf_op jit(solution)/shard_map/ppermute | solution.py:394
  15.0 3.4 %collective-permute-start.6 = (bf16[4,320,128]{2,1,0:T(8,128)(2,1)S(1)}, bf16[4,320,128]{2,1,0:T(8,128)(2,1)S(1)}, u32[]{:S(2)}, u32[]{:S(2)}) collective-permute-start(bf16[4,320,128]{2,1,0:T(8,128)(2,1)S(1)} %pack_value.1), channel_id=1, source_target_pairs={{0,2},{1,3},{2,4},{3,5},{4,6},{5,7},{6,8},{7,9},{8,10},{9,11},{10,... | collective-permute-start | bytes 983048 | tf_op jit(solution)/shard_map/ppermute | solution.py:391
  18.5 0.0 collective-permute-done.pix
  18.5 1.8 %ahead.1 = (bf16[2,8,640,128]{3,2,1,0:T(8,128)(2,1)S(1)}, bf16[1,640,128]{2,1,0:T(8,128)(2,1)S(1)}) custom-call(bf16[128,1536]{1,0:T(8,128)(2,1)S(1)} %collective-permute-done.pix, bf16[2,8,128,640]{3,2,1,0:T(8,128)(2,1)} %prior_hbm.1, bf16[1536,1280]{1,0:T(8,128)(2,1)S(1)} %get-tuple-element.32.we, f32[1280]{0:T(1024)S(1)} %get-tuple-element.33.gain_ref, ...), custom_call_target="tpu_custom_call" | custom-call | flops 1300000000 | bytes 1 | tf_op jit(solution)/shard_map/ahead/pallas_call | solution.py:428
  20.3 3.7 %collective-permute-done.1.sent_ref = bf16[3,640,128]{2,1,0:T(8,128)(2,1)S(1)} collective-permute-done((bf16[3,640,128]{2,1,0:T(8,128)(2,1)S(1)}, bf16[3,640,128]{2,1,0:T(8,128)(2,1)S(1)}, u32[]{:S(2)}, u32[]{:S(2)}) %collective-permute-start.1) | collective-permute-done | bytes 491552 | tf_op jit(solution)/shard_map/ppermute | solution.py:388
  24.1 0.1 collective-permute-start.2
  24.2 2.5 %collective-permute-start.10 = (bf16[2,640,128]{2,1,0:T(8,128)(2,1)S(1)}, bf16[2,640,128]{2,1,0:T(8,128)(2,1)S(1)}, u32[]{:S(2)}, u32[]{:S(2)}) collective-permute-start(bf16[2,640,128]{2,1,0:T(8,128)(2,1)S(1)} %get-tuple-element.48), channel_id=1, source_target_pairs={{0,2},{2,4},{4,6},{6,8},{8,10},{10,12},{12,14},{16,18},{18,20},{20... | collective-permute-start | bytes 983048 | tf_op jit(solution)/shard_map/ppermute | solution.py:391
  26.7 0.8 %score.1.far_own_ref = f32[4,9,8,128]{3,2,1,0:T(8,128)S(1)} custom-call(bf16[4,640,128]{2,1,0:T(8,128)(2,1)S(1)} %get-tuple-element.31.q_ref, bf16[3,640,128]{2,1,0:T(8,128)(2,1)S(1)} %collective-permute-done.1.sent_ref, bf16[2,8,640,128]{3,2,1,0:T(8,128)(2,1)S(1)} %get-tuple-element.35.ahead_ref, bf16[3,640,128]{2,1,0:T(8,128)(2,1)S(1)} %get-tuple-element.37.most_ref, ...), custom_call_target="tpu_custom_call" | custom-call | flops 1000000 | bytes 1 | tf_op jit(solution)/shard_map/score/pallas_call | solution.py:434
  27.5 0.1 collective-permute-start.3
  27.6 0.5 %collective-permute-start.7 = (bf16[1,640,128]{2,1,0:T(8,128)(2,1)S(1)}, bf16[1,640,128]{2,1,0:T(8,128)(2,1)S(1)}, u32[]{:S(2)}, u32[]{:S(2)}) collective-permute-start(bf16[1,640,128]{2,1,0:T(8,128)(2,1)S(1)} %get-tuple-element.44), channel_id=1, source_target_pairs={{0,1},{1,0},{2,3},{3,2},{4,5},{5,4},{6,7},{7,6},{8,9},{9,8},{10,11... | collective-permute-start | bytes 491528 | tf_op jit(solution)/shard_map/ppermute | solution.py:394
  28.1 2.3 %collective-permute-done.6.held_ref = bf16[4,320,128]{2,1,0:T(8,128)(2,1)S(1)} collective-permute-done((bf16[4,320,128]{2,1,0:T(8,128)(2,1)S(1)}, bf16[4,320,128]{2,1,0:T(8,128)(2,1)S(1)}, u32[]{:S(2)}, u32[]{:S(2)}) %collective-permute-start.6) | collective-permute-done | bytes 327712 | tf_op jit(solution)/shard_map/ppermute | solution.py:391
  30.4 0.1 collective-permute-start.8
  30.5 0.0 collective-permute-done.2.refs_0_
  30.5 0.5 %collective-permute-start.9 = (bf16[4,160,128]{2,1,0:T(8,128)(2,1)S(1)}, bf16[4,160,128]{2,1,0:T(8,128)(2,1)S(1)}, u32[]{:S(2)}, u32[]{:S(2)}) collective-permute-start(bf16[4,160,128]{2,1,0:T(8,128)(2,1)S(1)} %get-tuple-element.51), channel_id=1, source_target_pairs={{0,1},{1,0},{2,3},{3,2},{4,5},{5,4},{6,7},{7,6},{8,9},{9,8},{10,11... | collective-permute-start | bytes 491528 | tf_op jit(solution)/shard_map/ppermute | solution.py:394
  31.0 0.0 collective-permute-done.3.refs_1_
  31.0 0.7 %weight.1.w_ref = f32[4,9,8,128]{3,2,1,0:T(8,128)S(1)} custom-call(bf16[4,640,128]{2,1,0:T(8,128)(2,1)S(1)} %get-tuple-element.31.q_ref, bf16[2,8,640,128]{3,2,1,0:T(8,128)(2,1)S(1)} %get-tuple-element.35.ahead_ref, f32[4,9,8,128]{3,2,1,0:T(8,128)S(1)} %score.1.far_own_ref, bf16[2,640,128]{2,1,0:T(8,128)(2,1)S(1)} %collective-permute-done.2.refs_0_, ...), custom_call_target="tpu_custom_call" | custom-call | flops 1000000 | bytes 1 | tf_op jit(solution)/shard_map/weight/pallas_call | solution.py:449
  31.7 0.0 collective-permute-done.7.last_ref
  31.7 0.2 collective-permute-done.8.refs_0_
  31.9 0.2 collective-permute-done.9.refs_1_
  32.1 1.6 %mix.1 = (bf16[2,128,1280]{2,1,0:T(8,128)(2,1)S(1)}, f32[2,640,128]{2,1,0:T(8,128)S(1)}, bf16[2,640,128]{2,1,0:T(8,128)(2,1)S(1)}) custom-call(f32[4,9,8,128]{3,2,1,0:T(8,128)S(1)} %weight.1.w_ref, bf16[2,8,640,128]{3,2,1,0:T(8,128)(2,1)S(1)} %get-tuple-element.35.ahead_ref, bf16[4,320,128]{2,1,0:T(8,128)(2,1)S(1)} %collective-permute-done.6.held_ref, ...), custom_call_target="tpu_custom_call" | custom-call | flops 1000000 | bytes 1 | tf_op jit(solution)/shard_map/mix/pallas_call | solution.py:458
  33.7 0.3 collective-permute-done.10.even_ref
  34.0 1.5 %finish.1 = bf16[4,128,1280]{2,1,0:T(8,128)(2,1)} custom-call(f32[4,9,8,128]{3,2,1,0:T(8,128)S(1)} %weight.1.w_ref, bf16[2,640,128]{2,1,0:T(8,128)(2,1)S(1)} %get-tuple-element.47.odd_ref, bf16[2,640,128]{2,1,0:T(8,128)(2,1)S(1)} %collective-permute-done.10.even_ref, bf16[2,8,640,128]{3,2,1,0:T(8,128)(2,1)S(1)} %get-tuple-element.35.ahead_ref, ...), custom_call_target="tpu_custom_call" | custom-call | flops 1000000 | bytes 1 | tf_op jit(solution)/shard_map/finish/pallas_call | solution.py:464
  (3 shorter events, 0.1 us)
Async XLA Ops:
  1.0 17.4 %collective-permute-start = (bf16[128,1536]{1,0:T(8,128)(2,1)S(1)}, bf16[128,1536]{1,0:T(8,128)(2,1)S(1)}, u32[]{:S(2)}, u32[]{:S(2)}) collective-permute-start(bf16[128,1536]{1,0:T(8,128)(2,1)S(1)} %slice.13), channel_id=1, source_target_pairs={{0,2},{1,3},{2,4},{3,5},{4,6},{5,7},{6,8},{7,9},{8,10},{9,11},{10,... | collective-permute-start | bytes 1179656 | tf_op jit(solution)/shard_map/ppermute | solution.py:388
  9.0 15.1 %collective-permute-start.1 = (bf16[3,640,128]{2,1,0:T(8,128)(2,1)S(1)}, bf16[3,640,128]{2,1,0:T(8,128)(2,1)S(1)}, u32[]{:S(2)}, u32[]{:S(2)}) collective-permute-start(bf16[3,640,128]{2,1,0:T(8,128)(2,1)S(1)} %get-tuple-element.37.most_ref), channel_id=1, source_target_pairs={{0,2},{1,3},{2,4},{3,5},{4,6},{5,7},{6,8},{7,9},{8,10},{9,11},{10,... | collective-permute-start | bytes 1474568 | tf_op jit(solution)/shard_map/ppermute | solution.py:388
  12.8 1.7 %collective-permute-start.4 = (bf16[2,640,128]{2,1,0:T(8,128)(2,1)S(1)}, bf16[2,640,128]{2,1,0:T(8,128)(2,1)S(1)}, u32[]{:S(2)}, u32[]{:S(2)}) collective-permute-start(bf16[2,640,128]{2,1,0:T(8,128)(2,1)S(1)} %get-tuple-element.42.refs_0_.refs_4_), channel_id=1, source_target_pairs={{0,1},{1,0},{2,3},{3,2},{4,5},{5,4},{6,7},{7,6},{8,9},{9,8},{10,11... | collective-permute-start | bytes 983048 | tf_op jit(solution)/shard_map/ppermute | solution.py:394
  12.9 2.1 %collective-permute-start.5 = (bf16[2,640,128]{2,1,0:T(8,128)(2,1)S(1)}, bf16[2,640,128]{2,1,0:T(8,128)(2,1)S(1)}, u32[]{:S(2)}, u32[]{:S(2)}) collective-permute-start(bf16[2,640,128]{2,1,0:T(8,128)(2,1)S(1)} %get-tuple-element.43.refs_1_.refs_5_), channel_id=1, source_target_pairs={{0,1},{1,0},{2,3},{3,2},{4,5},{5,4},{6,7},{7,6},{8,9},{9,8},{10,11... | collective-permute-start | bytes 983048 | tf_op jit(solution)/shard_map/ppermute | solution.py:394
  15.0 15.4 %collective-permute-start.6 = (bf16[4,320,128]{2,1,0:T(8,128)(2,1)S(1)}, bf16[4,320,128]{2,1,0:T(8,128)(2,1)S(1)}, u32[]{:S(2)}, u32[]{:S(2)}) collective-permute-start(bf16[4,320,128]{2,1,0:T(8,128)(2,1)S(1)} %pack_value.1), channel_id=1, source_target_pairs={{0,2},{1,3},{2,4},{3,5},{4,6},{5,7},{6,8},{7,9},{8,10},{9,11},{10,... | collective-permute-start | bytes 983048 | tf_op jit(solution)/shard_map/ppermute | solution.py:391
  24.1 6.4 %collective-permute-start.2 = (bf16[2,640,128]{2,1,0:T(8,128)(2,1)S(1)}, bf16[2,640,128]{2,1,0:T(8,128)(2,1)S(1)}, u32[]{:S(2)}, u32[]{:S(2)}) collective-permute-start(bf16[2,640,128]{2,1,0:T(8,128)(2,1)S(1)} %get-tuple-element.40), channel_id=1, source_target_pairs={{0,1},{1,0},{2,3},{3,2},{4,5},{5,4},{6,7},{7,6},{8,9},{9,8},{10,11... | collective-permute-start | bytes 983048 | tf_op jit(solution)/shard_map/ppermute | solution.py:394
  24.2 9.9 %collective-permute-start.10 = (bf16[2,640,128]{2,1,0:T(8,128)(2,1)S(1)}, bf16[2,640,128]{2,1,0:T(8,128)(2,1)S(1)}, u32[]{:S(2)}, u32[]{:S(2)}) collective-permute-start(bf16[2,640,128]{2,1,0:T(8,128)(2,1)S(1)} %get-tuple-element.48), channel_id=1, source_target_pairs={{0,2},{2,4},{4,6},{6,8},{8,10},{10,12},{12,14},{16,18},{18,20},{20... | collective-permute-start | bytes 983048 | tf_op jit(solution)/shard_map/ppermute | solution.py:391
  27.5 3.5 %collective-permute-start.3 = (bf16[2,640,128]{2,1,0:T(8,128)(2,1)S(1)}, bf16[2,640,128]{2,1,0:T(8,128)(2,1)S(1)}, u32[]{:S(2)}, u32[]{:S(2)}) collective-permute-start(bf16[2,640,128]{2,1,0:T(8,128)(2,1)S(1)} %get-tuple-element.41), channel_id=1, source_target_pairs={{0,1},{1,0},{2,3},{3,2},{4,5},{5,4},{6,7},{7,6},{8,9},{9,8},{10,11... | collective-permute-start | bytes 983048 | tf_op jit(solution)/shard_map/ppermute | solution.py:394
  27.6 4.1 %collective-permute-start.7 = (bf16[1,640,128]{2,1,0:T(8,128)(2,1)S(1)}, bf16[1,640,128]{2,1,0:T(8,128)(2,1)S(1)}, u32[]{:S(2)}, u32[]{:S(2)}) collective-permute-start(bf16[1,640,128]{2,1,0:T(8,128)(2,1)S(1)} %get-tuple-element.44), channel_id=1, source_target_pairs={{0,1},{1,0},{2,3},{3,2},{4,5},{5,4},{6,7},{7,6},{8,9},{9,8},{10,11... | collective-permute-start | bytes 491528 | tf_op jit(solution)/shard_map/ppermute | solution.py:394
  30.4 1.5 %collective-permute-start.8 = (bf16[4,160,128]{2,1,0:T(8,128)(2,1)S(1)}, bf16[4,160,128]{2,1,0:T(8,128)(2,1)S(1)}, u32[]{:S(2)}, u32[]{:S(2)}) collective-permute-start(bf16[4,160,128]{2,1,0:T(8,128)(2,1)S(1)} %get-tuple-element.52), channel_id=1, source_target_pairs={{0,1},{1,0},{2,3},{3,2},{4,5},{5,4},{6,7},{7,6},{8,9},{9,8},{10,11... | collective-permute-start | bytes 491528 | tf_op jit(solution)/shard_map/ppermute | solution.py:394
  30.5 1.6 %collective-permute-start.9 = (bf16[4,160,128]{2,1,0:T(8,128)(2,1)S(1)}, bf16[4,160,128]{2,1,0:T(8,128)(2,1)S(1)}, u32[]{:S(2)}, u32[]{:S(2)}) collective-permute-start(bf16[4,160,128]{2,1,0:T(8,128)(2,1)S(1)} %get-tuple-element.51), channel_id=1, source_target_pairs={{0,1},{1,0},{2,3},{3,2},{4,5},{5,4},{6,7},{7,6},{8,9},{9,8},{10,11... | collective-permute-start | bytes 491528 | tf_op jit(solution)/shard_map/ppermute | solution.py:394

commit v2 on v1

--- a/solution.py
+++ b/solution.py
@@ -327,7 +327,7 @@
                 mix[t - start, part, :] = sums[t].astype(BF)
         return carry
 
-    lax.fori_loop(0, HEADS, head, 0)
+    lax.fori_loop(0, HEADS, head, 0, unroll=4)
     for t in range(start, tub):
         done_ref[t - start] = finished(mix[t - start], e_ref.at[t], wo_ref)
 

time: 36 us -> 35.9 us (level)
  no operation moved by 1% of the time
where the time goes in v2:
time: 35.9 us; the launch traced here: 35.6 us
  Pallas kernels  16.2 us (45%)
  starting transfers between devices  10.9 us (30%)
  waiting for transfers between devices  8.37 us (23%)
    pallas_call x1, Pallas kernels, body(): call(front_kernel, 'front', 24, (shape((rows, width)), shape((rows, width...  6.37 us
    ppermute x2, starting transfers between devices, shift(): lax.ppermute(value, 'tm', [(i, i + 2) for i in range(start, count - 2, st...  5.96 us
    ppermute x2, waiting for transfers between devices, ring(): lax.ppermute(value, 'tm', [(i, (i + 2) % count) for i in range(count)])  3.73 us
    ppermute x2, starting transfers between devices, ring(): lax.ppermute(value, 'tm', [(i, (i + 2) % count) for i in range(count)])  3.14 us
    ppermute x2, waiting for transfers between devices, shift(): lax.ppermute(value, 'tm', [(i, i + 2) for i in range(start, count - 2, st...  2.64 us
    pallas_call x1, Pallas kernels, body(): call(second_kernel, 'second', 16, (shape(start), shape(turned), *[shape((...  2.29 us
    ppermute x7, waiting for transfers between devices, swap(): return lax.ppermute(value, 'tm', [(i, i ^ 1) for i in range(count)])  2 us
    pallas_call x1, Pallas kernels, body(): call(ahead_kernel, 'ahead', 24, (shape((2, reach, inner, pat)), shape(res...  1.84 us
  transfers between devices with their start and end apart: 11, of which 7 were waited for; matrix products, arithmetic and copies ran while one was open for 0% of the time, Pallas kernels for 38%

profile of v2, /device:TPU:10, one launch (start us, length us, event | category | flops | bytes accessed | tf_op | source)
XLA Modules:
  0.0 35.6 jit_solution(12504277607396356224)
XLA Ops:
  0.0 1.0 %slice.13 = bf16[128,1536]{1,0:T(8,128)(2,1)S(1)} custom-call(bf16[4,128,1536]{2,1,0:T(8,128)(2,1)} %pix_hbm.1), custom_call_target="tpu_custom_call" | custom-call | flops 1000000 | bytes 1 | tf_op jit(solution)/shard_map/slice/pallas_call | solution.py:397
  1.0 1.6 %collective-permute-start = (bf16[128,1536]{1,0:T(8,128)(2,1)S(1)}, bf16[128,1536]{1,0:T(8,128)(2,1)S(1)}, u32[]{:S(2)}, u32[]{:S(2)}) collective-permute-start(bf16[128,1536]{1,0:T(8,128)(2,1)S(1)} %slice.13), channel_id=1, source_target_pairs={{0,2},{1,3},{2,4},{3,5},{4,6},{5,7},{6,8},{7,9},{8,10},{9,11},{10,... | collective-permute-start | bytes 1179656 | tf_op jit(solution)/shard_map/ppermute | solution.py:388
  2.6 6.4 %front.1 = (bf16[512,1280]{1,0:T(8,128)(2,1)S(1)}, bf16[512,1280]{1,0:T(8,128)(2,1)S(1)}, bf16[3,640,128]{2,1,0:T(8,128)(2,1)S(1)}, bf16[1,640,128]{2,1,0:T(8,12...) custom-call(bf16[512,1536]{1,0:T(8,128)(2,1)} %bitcast.4, ...), custom_call_target="tpu_custom_call" | custom-call | flops 36999999488 | bytes 1 | tf_op jit(solution)/shard_map/front/pallas_call | solution.py:401
  9.0 1.6 %collective-permute-start.1 = (bf16[3,640,128]{2,1,0:T(8,128)(2,1)S(1)}, bf16[3,640,128]{2,1,0:T(8,128)(2,1)S(1)}, u32[]{:S(2)}, u32[]{:S(2)}) collective-permute-start(bf16[3,640,128]{2,1,0:T(8,128)(2,1)S(1)} %get-tuple-element.37.most_ref), channel_id=1, source_target_pairs={{0,2},{1,3},{2,4},{3,5},{4,6},{5,7},{6,8},{7,9},{8,10},{9,11},{10,... | collective-permute-start | bytes 1474568 | tf_op jit(solution)/shard_map/ppermute | solution.py:388
  10.5 2.3 %second.1 = (bf16[2,640,128]{2,1,0:T(8,128)(2,1)S(1)}, bf16[4,640,128]{2,1,0:T(8,128)(2,1)S(1)}, bf16[2,640,128]{2,1,0:T(8,128)(2,1)S(1)}, bf16[2,640,128]{2,1,0:T(8,128)(2,1)S(1)}) custom-call(bf16[512,1280]{1,0:T(8,128)(2,1)S(1)} %get-tuple-element.28.nor, bf16[1280,640]{1,0:T(8,128)(2,1)S(1)} %get-tuple-element.29.wv, ...), custom_call_target="tpu_custom_call" | custom-call | flops 1000000 | bytes 1 | tf_op jit(solution)/shard_map/second/pallas_call | solution.py:415
  12.8 0.1 collective-permute-start.4
  12.9 0.5 %collective-permute-start.5 = (bf16[2,640,128]{2,1,0:T(8,128)(2,1)S(1)}, bf16[2,640,128]{2,1,0:T(8,128)(2,1)S(1)}, u32[]{:S(2)}, u32[]{:S(2)}) collective-permute-start(bf16[2,640,128]{2,1,0:T(8,128)(2,1)S(1)} %get-tuple-element.43.refs_1_.refs_5_), channel_id=1, source_target_pairs={{0,1},{1,0},{2,3},{3,2},{4,5},{5,4},{6,7},{7,6},{8,9},{9,8},{10,11... | collective-permute-start | bytes 983048 | tf_op jit(solution)/shard_map/ppermute | solution.py:394
  13.4 1.1 %collective-permute-done.4.refs_2_ = bf16[2,640,128]{2,1,0:T(8,128)(2,1)S(1)} collective-permute-done((bf16[2,640,128]{2,1,0:T(8,128)(2,1)S(1)}, bf16[2,640,128]{2,1,0:T(8,128)(2,1)S(1)}, u32[]{:S(2)}, u32[]{:S(2)}) %collective-permute-start.4) | collective-permute-done | bytes 327712 | tf_op jit(solution)/shard_map/ppermute | solution.py:394
  14.5 0.5 %collective-permute-done.5.refs_3_ = bf16[2,640,128]{2,1,0:T(8,128)(2,1)S(1)} collective-permute-done((bf16[2,640,128]{2,1,0:T(8,128)(2,1)S(1)}, bf16[2,640,128]{2,1,0:T(8,128)(2,1)S(1)}, u32[]{:S(2)}, u32[]{:S(2)}) %collective-permute-start.5) | collective-permute-done | bytes 327712 | tf_op jit(solution)/shard_map/ppermute | solution.py:394
  15.0 3.4 %collective-permute-start.6 = (bf16[4,320,128]{2,1,0:T(8,128)(2,1)S(1)}, bf16[4,320,128]{2,1,0:T(8,128)(2,1)S(1)}, u32[]{:S(2)}, u32[]{:S(2)}) collective-permute-start(bf16[4,320,128]{2,1,0:T(8,128)(2,1)S(1)} %pack_value.1), channel_id=1, source_target_pairs={{0,2},{1,3},{2,4},{3,5},{4,6},{5,7},{6,8},{7,9},{8,10},{9,11},{10,... | collective-permute-start | bytes 983048 | tf_op jit(solution)/shard_map/ppermute | solution.py:391
  18.5 0.0 collective-permute-done.pix
  18.5 1.8 %ahead.1 = (bf16[2,8,640,128]{3,2,1,0:T(8,128)(2,1)S(1)}, bf16[1,640,128]{2,1,0:T(8,128)(2,1)S(1)}) custom-call(bf16[128,1536]{1,0:T(8,128)(2,1)S(1)} %collective-permute-done.pix, bf16[2,8,128,640]{3,2,1,0:T(8,128)(2,1)} %prior_hbm.1, bf16[1536,1280]{1,0:T(8,128)(2,1)S(1)} %get-tuple-element.32.we, f32[1280]{0:T(1024)S(1)} %get-tuple-element.33.gain_ref, ...), custom_call_target="tpu_custom_call" | custom-call | flops 1300000000 | bytes 1 | tf_op jit(solution)/shard_map/ahead/pallas_call | solution.py:428
  20.3 3.7 %collective-permute-done.1.sent_ref = bf16[3,640,128]{2,1,0:T(8,128)(2,1)S(1)} collective-permute-done((bf16[3,640,128]{2,1,0:T(8,128)(2,1)S(1)}, bf16[3,640,128]{2,1,0:T(8,128)(2,1)S(1)}, u32[]{:S(2)}, u32[]{:S(2)}) %collective-permute-start.1) | collective-permute-done | bytes 491552 | tf_op jit(solution)/shard_map/ppermute | solution.py:388
  24.1 0.1 collective-permute-start.2
  24.2 2.5 %collective-permute-start.10 = (bf16[2,640,128]{2,1,0:T(8,128)(2,1)S(1)}, bf16[2,640,128]{2,1,0:T(8,128)(2,1)S(1)}, u32[]{:S(2)}, u32[]{:S(2)}) collective-permute-start(bf16[2,640,128]{2,1,0:T(8,128)(2,1)S(1)} %get-tuple-element.48), channel_id=1, source_target_pairs={{0,2},{2,4},{4,6},{6,8},{8,10},{10,12},{12,14},{16,18},{18,20},{20... | collective-permute-start | bytes 983048 | tf_op jit(solution)/shard_map/ppermute | solution.py:391
  26.7 0.8 %score.1.far_own_ref = f32[4,9,8,128]{3,2,1,0:T(8,128)S(1)} custom-call(bf16[4,640,128]{2,1,0:T(8,128)(2,1)S(1)} %get-tuple-element.31.q_ref, bf16[3,640,128]{2,1,0:T(8,128)(2,1)S(1)} %collective-permute-done.1.sent_ref, bf16[2,8,640,128]{3,2,1,0:T(8,128)(2,1)S(1)} %get-tuple-element.35.ahead_ref, bf16[3,640,128]{2,1,0:T(8,128)(2,1)S(1)} %get-tuple-element.37.most_ref, ...), custom_call_target="tpu_custom_call" | custom-call | flops 1000000 | bytes 1 | tf_op jit(solution)/shard_map/score/pallas_call | solution.py:434
  27.5 0.1 collective-permute-start.3
  27.6 0.5 %collective-permute-start.7 = (bf16[1,640,128]{2,1,0:T(8,128)(2,1)S(1)}, bf16[1,640,128]{2,1,0:T(8,128)(2,1)S(1)}, u32[]{:S(2)}, u32[]{:S(2)}) collective-permute-start(bf16[1,640,128]{2,1,0:T(8,128)(2,1)S(1)} %get-tuple-element.44), channel_id=1, source_target_pairs={{0,1},{1,0},{2,3},{3,2},{4,5},{5,4},{6,7},{7,6},{8,9},{9,8},{10,11... | collective-permute-start | bytes 491528 | tf_op jit(solution)/shard_map/ppermute | solution.py:394
  28.1 2.3 %collective-permute-done.6.held_ref = bf16[4,320,128]{2,1,0:T(8,128)(2,1)S(1)} collective-permute-done((bf16[4,320,128]{2,1,0:T(8,128)(2,1)S(1)}, bf16[4,320,128]{2,1,0:T(8,128)(2,1)S(1)}, u32[]{:S(2)}, u32[]{:S(2)}) %collective-permute-start.6) | collective-permute-done | bytes 327712 | tf_op jit(solution)/shard_map/ppermute | solution.py:391
  30.4 0.1 collective-permute-start.8
  30.5 0.0 collective-permute-done.2.refs_0_
  30.5 0.5 %collective-permute-start.9 = (bf16[4,160,128]{2,1,0:T(8,128)(2,1)S(1)}, bf16[4,160,128]{2,1,0:T(8,128)(2,1)S(1)}, u32[]{:S(2)}, u32[]{:S(2)}) collective-permute-start(bf16[4,160,128]{2,1,0:T(8,128)(2,1)S(1)} %get-tuple-element.51), channel_id=1, source_target_pairs={{0,1},{1,0},{2,3},{3,2},{4,5},{5,4},{6,7},{7,6},{8,9},{9,8},{10,11... | collective-permute-start | bytes 491528 | tf_op jit(solution)/shard_map/ppermute | solution.py:394
  31.0 0.0 collective-permute-done.3.refs_1_
  31.0 0.7 %weight.1.w_ref = f32[4,9,8,128]{3,2,1,0:T(8,128)S(1)} custom-call(bf16[4,640,128]{2,1,0:T(8,128)(2,1)S(1)} %get-tuple-element.31.q_ref, bf16[2,8,640,128]{3,2,1,0:T(8,128)(2,1)S(1)} %get-tuple-element.35.ahead_ref, f32[4,9,8,128]{3,2,1,0:T(8,128)S(1)} %score.1.far_own_ref, bf16[2,640,128]{2,1,0:T(8,128)(2,1)S(1)} %collective-permute-done.2.refs_0_, ...), custom_call_target="tpu_custom_call" | custom-call | flops 1000000 | bytes 1 | tf_op jit(solution)/shard_map/weight/pallas_call | solution.py:449
  31.7 0.0 collective-permute-done.7.last_ref
  31.7 0.2 collective-permute-done.8.refs_0_
  31.9 0.2 collective-permute-done.9.refs_1_
  32.1 1.6 %mix.1 = (bf16[2,128,1280]{2,1,0:T(8,128)(2,1)S(1)}, f32[2,640,128]{2,1,0:T(8,128)S(1)}, bf16[2,640,128]{2,1,0:T(8,128)(2,1)S(1)}) custom-call(f32[4,9,8,128]{3,2,1,0:T(8,128)S(1)} %weight.1.w_ref, bf16[2,8,640,128]{3,2,1,0:T(8,128)(2,1)S(1)} %get-tuple-element.35.ahead_ref, bf16[4,320,128]{2,1,0:T(8,128)(2,1)S(1)} %collective-permute-done.6.held_ref, ...), custom_call_target="tpu_custom_call" | custom-call | flops 1000000 | bytes 1 | tf_op jit(solution)/shard_map/mix/pallas_call | solution.py:458
  33.7 0.4 %collective-permute-done.10.even_ref = bf16[2,640,128]{2,1,0:T(8,128)(2,1)S(1)} collective-permute-done((bf16[2,640,128]{2,1,0:T(8,128)(2,1)S(1)}, bf16[2,640,128]{2,1,0:T(8,128)(2,1)S(1)}, u32[]{:S(2)}, u32[]{:S(2)}) %collective-permute-start.10) | collective-permute-done | bytes 327712 | tf_op jit(solution)/shard_map/ppermute | solution.py:391
  34.0 1.5 %finish.1 = bf16[4,128,1280]{2,1,0:T(8,128)(2,1)} custom-call(f32[4,9,8,128]{3,2,1,0:T(8,128)S(1)} %weight.1.w_ref, bf16[2,640,128]{2,1,0:T(8,128)(2,1)S(1)} %get-tuple-element.47.odd_ref, bf16[2,640,128]{2,1,0:T(8,128)(2,1)S(1)} %collective-permute-done.10.even_ref, bf16[2,8,640,128]{3,2,1,0:T(8,128)(2,1)S(1)} %get-tuple-element.35.ahead_ref, ...), custom_call_target="tpu_custom_call" | custom-call | flops 1000000 | bytes 1 | tf_op jit(solution)/shard_map/finish/pallas_call | solution.py:464
  (3 shorter events, 0.1 us)
Async XLA Ops:
  1.0 17.4 %collective-permute-start = (bf16[128,1536]{1,0:T(8,128)(2,1)S(1)}, bf16[128,1536]{1,0:T(8,128)(2,1)S(1)}, u32[]{:S(2)}, u32[]{:S(2)}) collective-permute-start(bf16[128,1536]{1,0:T(8,128)(2,1)S(1)} %slice.13), channel_id=1, source_target_pairs={{0,2},{1,3},{2,4},{3,5},{4,6},{5,7},{6,8},{7,9},{8,10},{9,11},{10,... | collective-permute-start | bytes 1179656 | tf_op jit(solution)/shard_map/ppermute | solution.py:388
  9.0 15.1 %collective-permute-start.1 = (bf16[3,640,128]{2,1,0:T(8,128)(2,1)S(1)}, bf16[3,640,128]{2,1,0:T(8,128)(2,1)S(1)}, u32[]{:S(2)}, u32[]{:S(2)}) collective-permute-start(bf16[3,640,128]{2,1,0:T(8,128)(2,1)S(1)} %get-tuple-element.37.most_ref), channel_id=1, source_target_pairs={{0,2},{1,3},{2,4},{3,5},{4,6},{5,7},{6,8},{7,9},{8,10},{9,11},{10,... | collective-permute-start | bytes 1474568 | tf_op jit(solution)/shard_map/ppermute | solution.py:388
  12.8 1.7 %collective-permute-start.4 = (bf16[2,640,128]{2,1,0:T(8,128)(2,1)S(1)}, bf16[2,640,128]{2,1,0:T(8,128)(2,1)S(1)}, u32[]{:S(2)}, u32[]{:S(2)}) collective-permute-start(bf16[2,640,128]{2,1,0:T(8,128)(2,1)S(1)} %get-tuple-element.42.refs_0_.refs_4_), channel_id=1, source_target_pairs={{0,1},{1,0},{2,3},{3,2},{4,5},{5,4},{6,7},{7,6},{8,9},{9,8},{10,11... | collective-permute-start | bytes 983048 | tf_op jit(solution)/shard_map/ppermute | solution.py:394
  12.9 2.1 %collective-permute-start.5 = (bf16[2,640,128]{2,1,0:T(8,128)(2,1)S(1)}, bf16[2,640,128]{2,1,0:T(8,128)(2,1)S(1)}, u32[]{:S(2)}, u32[]{:S(2)}) collective-permute-start(bf16[2,640,128]{2,1,0:T(8,128)(2,1)S(1)} %get-tuple-element.43.refs_1_.refs_5_), channel_id=1, source_target_pairs={{0,1},{1,0},{2,3},{3,2},{4,5},{5,4},{6,7},{7,6},{8,9},{9,8},{10,11... | collective-permute-start | bytes 983048 | tf_op jit(solution)/shard_map/ppermute | solution.py:394
  15.0 15.4 %collective-permute-start.6 = (bf16[4,320,128]{2,1,0:T(8,128)(2,1)S(1)}, bf16[4,320,128]{2,1,0:T(8,128)(2,1)S(1)}, u32[]{:S(2)}, u32[]{:S(2)}) collective-permute-start(bf16[4,320,128]{2,1,0:T(8,128)(2,1)S(1)} %pack_value.1), channel_id=1, source_target_pairs={{0,2},{1,3},{2,4},{3,5},{4,6},{5,7},{6,8},{7,9},{8,10},{9,11},{10,... | collective-permute-start | bytes 983048 | tf_op jit(solution)/shard_map/ppermute | solution.py:391
  24.1 6.4 %collective-permute-start.2 = (bf16[2,640,128]{2,1,0:T(8,128)(2,1)S(1)}, bf16[2,640,128]{2,1,0:T(8,128)(2,1)S(1)}, u32[]{:S(2)}, u32[]{:S(2)}) collective-permute-start(bf16[2,640,128]{2,1,0:T(8,128)(2,1)S(1)} %get-tuple-element.40), channel_id=1, source_target_pairs={{0,1},{1,0},{2,3},{3,2},{4,5},{5,4},{6,7},{7,6},{8,9},{9,8},{10,11... | collective-permute-start | bytes 983048 | tf_op jit(solution)/shard_map/ppermute | solution.py:394
  24.2 9.9 %collective-permute-start.10 = (bf16[2,640,128]{2,1,0:T(8,128)(2,1)S(1)}, bf16[2,640,128]{2,1,0:T(8,128)(2,1)S(1)}, u32[]{:S(2)}, u32[]{:S(2)}) collective-permute-start(bf16[2,640,128]{2,1,0:T(8,128)(2,1)S(1)} %get-tuple-element.48), channel_id=1, source_target_pairs={{0,2},{2,4},{4,6},{6,8},{8,10},{10,12},{12,14},{16,18},{18,20},{20... | collective-permute-start | bytes 983048 | tf_op jit(solution)/shard_map/ppermute | solution.py:391
  27.5 3.5 %collective-permute-start.3 = (bf16[2,640,128]{2,1,0:T(8,128)(2,1)S(1)}, bf16[2,640,128]{2,1,0:T(8,128)(2,1)S(1)}, u32[]{:S(2)}, u32[]{:S(2)}) collective-permute-start(bf16[2,640,128]{2,1,0:T(8,128)(2,1)S(1)} %get-tuple-element.41), channel_id=1, source_target_pairs={{0,1},{1,0},{2,3},{3,2},{4,5},{5,4},{6,7},{7,6},{8,9},{9,8},{10,11... | collective-permute-start | bytes 983048 | tf_op jit(solution)/shard_map/ppermute | solution.py:394
  27.6 4.1 %collective-permute-start.7 = (bf16[1,640,128]{2,1,0:T(8,128)(2,1)S(1)}, bf16[1,640,128]{2,1,0:T(8,128)(2,1)S(1)}, u32[]{:S(2)}, u32[]{:S(2)}) collective-permute-start(bf16[1,640,128]{2,1,0:T(8,128)(2,1)S(1)} %get-tuple-element.44), channel_id=1, source_target_pairs={{0,1},{1,0},{2,3},{3,2},{4,5},{5,4},{6,7},{7,6},{8,9},{9,8},{10,11... | collective-permute-start | bytes 491528 | tf_op jit(solution)/shard_map/ppermute | solution.py:394
  30.4 1.5 %collective-permute-start.8 = (bf16[4,160,128]{2,1,0:T(8,128)(2,1)S(1)}, bf16[4,160,128]{2,1,0:T(8,128)(2,1)S(1)}, u32[]{:S(2)}, u32[]{:S(2)}) collective-permute-start(bf16[4,160,128]{2,1,0:T(8,128)(2,1)S(1)} %get-tuple-element.52), channel_id=1, source_target_pairs={{0,1},{1,0},{2,3},{3,2},{4,5},{5,4},{6,7},{7,6},{8,9},{9,8},{10,11... | collective-permute-start | bytes 491528 | tf_op jit(solution)/shard_map/ppermute | solution.py:394
  30.5 1.6 %collective-permute-start.9 = (bf16[4,160,128]{2,1,0:T(8,128)(2,1)S(1)}, bf16[4,160,128]{2,1,0:T(8,128)(2,1)S(1)}, u32[]{:S(2)}, u32[]{:S(2)}) collective-permute-start(bf16[4,160,128]{2,1,0:T(8,128)(2,1)S(1)} %get-tuple-element.51), channel_id=1, source_target_pairs={{0,1},{1,0},{2,3},{3,2},{4,5},{5,4},{6,7},{7,6},{8,9},{9,8},{10,11... | collective-permute-start | bytes 491528 | tf_op jit(solution)/shard_map/ppermute | solution.py:394
